TPU v7x, 128 devices: a whole 4x4x4 slice. The times are simulated.
128 devices in a mesh: dp: 4 (over z_lo, core), row: 8 (over y, z_hi), col: 4 (over x).
Axes of the slice: x: 4, y: 4, z: 4 (z_hi: 2, z_lo: 2; z = z_hi * 2 + z_lo), core: 2. Of those that a mesh axis runs over, the one named last changes fastest.
Arguments:
- layer_input: bfloat16 [4096, 8192], P(('dp', 'col'), 'row'), may hold values from -6 to 6
- hidden_grad: bfloat16 [4096, 14336], P(('dp', 'row'), 'col'), may hold values from -4 to 4
- gate_pre: bfloat16 [4096, 14336], P(('dp', 'row'), 'col'), may hold values from -10 to 10
- up_pre: bfloat16 [4096, 14336], P(('dp', 'row'), 'col'), may hold values from -6 to 6
- gate_weight: bfloat16 [8192, 14336], P('row', 'col'), may hold values from -0.0625 to 0.0625
- up_weight: bfloat16 [8192, 14336], P('row', 'col'), may hold values from -0.0625 to 0.0625
Outputs:
- input_grad: bfloat16 [4096, 8192], P(('dp', 'col'), 'row')
- gate_weight_grad: bfloat16 [8192, 14336], P(('row', 'dp'), 'col')
- up_weight_grad: bfloat16 [8192, 14336], P(('row', 'dp'), 'col')
All inputs are finite; a program needn't handle non-finite values.
Results may differ from a plain program's by a relative error of at most 0.015.
Values may be sent and summed in bfloat16 or wider, within the bound.
No kernel may reach another device: no remote copies, remote signals or barrier semaphores. Data moves between devices by JAX's collectives and lax.ppermute only.
A program may use at most 256 MiB of HBM per device.

v0:
```python
import jax
import jax.numpy as jnp
from jax import lax
from jax.sharding import PartitionSpec as P


def weight_term(first_rows, second_rows):
    return lax.dot_general(
        first_rows, second_rows, (((0,), (0,)), ((), ())), preferred_element_type=jnp.float32
    )


def body(layer_input, hidden_grad, gate_pre, up_pre, gate_weight, up_weight):
    gate_value = gate_pre.astype(jnp.float32)
    sigmoid_gate = jax.nn.sigmoid(gate_value)
    grad_value = hidden_grad.astype(jnp.float32)
    gate_grad = (
        grad_value
        * up_pre.astype(jnp.float32)
        * sigmoid_gate
        * (1.0 + gate_value * (1.0 - sigmoid_gate))
    ).astype(jnp.bfloat16)
    up_grad = (grad_value * gate_value * sigmoid_gate).astype(jnp.bfloat16)
    group_gate, group_up = (
        lax.all_gather(gate_grad, "row", axis=0, tiled=True),
        lax.all_gather(up_grad, "row", axis=0, tiled=True),
    )
    group_input = lax.all_gather(layer_input, "col", axis=0, tiled=True)
    inverse_groups = 1.0 / lax.axis_size("dp")
    gate_partial = weight_term(group_input, group_gate)
    up_partial = weight_term(group_input, group_up)
    gate_total, up_total = (
        lax.psum_scatter(
            gate_partial.astype(jnp.bfloat16), "dp", scatter_dimension=0, tiled=True
        ).astype(jnp.float32),
        lax.psum_scatter(
            up_partial.astype(jnp.bfloat16), "dp", scatter_dimension=0, tiled=True
        ).astype(jnp.float32),
    )
    partial_value = lax.dot_general(
        group_gate, gate_weight, (((1,), (1,)), ((), ())), preferred_element_type=jnp.float32
    )
    input_sum = lax.psum_scatter(
        (
            partial_value
            + lax.dot_general(
                group_up, up_weight, (((1,), (1,)), ((), ())), preferred_element_type=jnp.float32
            )
        ).astype(jnp.bfloat16),
        "col",
        scatter_dimension=0,
        tiled=True,
    )
    gate_weight_grad = (gate_total * inverse_groups).astype(jnp.bfloat16)
    up_weight_grad = (up_total * inverse_groups).astype(jnp.bfloat16)
    return (input_sum, gate_weight_grad, up_weight_grad)


def solution(mesh):
    return jax.shard_map(
        body,
        mesh=mesh,
        in_specs=(
            P(("dp", "col"), "row"),
            P(("dp", "row"), "col"),
            P(("dp", "row"), "col"),
            P(("dp", "row"), "col"),
            P("row", "col"),
            P("row", "col"),
        ),
        out_specs=(P(("dp", "col"), "row"), P(("row", "dp"), "col"), P(("row", "dp"), "col")),
        check_vma=False,
    )
```

profile of v0, /device:TPU:1, one launch (start us, length us, event | category | flops | bytes accessed | tf_op | source)
XLA Modules:
  0.0 431.9 jit_solution(15393429837099100656)
XLA Ops:
  7.2 0.0 all-gather.8.cloned.1.call-start
  7.2 0.7 all-gather.8.cloned.1.call-update
  7.9 0.0 all-gather.6.cloned.1.call-start
  7.9 3.9 fusion.10
  11.8 0.0 all-gather.6.cloned.1.call-update
  11.9 0.0 all-gather.4.cloned.1.call-start
  11.9 0.7 all-gather.4.cloned.1.call-update
  12.6 0.0 reduce-scatter.8.cloned.1.call-start
  12.7 31.1 %all-gather.8.cloned.1.call-done = bf16[1024,1024]{1,0:T(8,128)(2,1)} async-done(((bf16[256,1024]{1,0:T(8,128)(2,1)}), bf16[1024,1024]{1,0:T(8,128)(2,1)}) %all-gather.8.cloned.1.call-update) | async-done | bytes 2097168 | tf_op jit(solution)/shard_map/all_gather | solution.py:28
  43.7 101.9 %all-gather.6.cloned.1.call-done = bf16[1024,3584]{1,0:T(8,128)(2,1)} async-done(((bf16[128,3584]{1,0:T(8,128)(2,1)}), bf16[1024,3584]{1,0:T(8,128)(2,1)}) %all-gather.6.cloned.1.call-update) | async-done | bytes 7340048 | tf_op jit(solution)/shard_map/all_gather | solution.py:26
  145.6 12.6 %fusion.1 = bf16[1024,3584]{0,1:T(8,128)(2,1)} fusion(bf16[1024,3584]{1,0:T(8,128)(2,1)} %all-gather.6.cloned.1.call-done, bf16[1024,1024]{1,0:T(8,128)(2,1)} %all-gather.8.cloned.1.call-done), kind=kOutput, calls=%fused_computation.3 | convolution fusion | flops 7519862784 | bytes 16777216 | tf_op jit(solution)/shard_map/dot_general | solution.py:8
  158.3 0.0 copy-start
  158.3 0.0 reduce-scatter.8.cloned.1.call-update
  158.3 0.0 reduce-scatter.6.cloned.1.call-start
  158.3 87.3 %all-gather.4.cloned.1.call-done = bf16[1024,3584]{1,0:T(8,128)(2,1)} async-done(((bf16[128,3584]{1,0:T(8,128)(2,1)}), bf16[1024,3584]{1,0:T(8,128)(2,1)}) %all-gather.4.cloned.1.call-update) | async-done | bytes 7340048 | tf_op jit(solution)/shard_map/all_gather | solution.py:25
  245.6 0.0 copy-done
  245.6 13.0 %fusion = bf16[1024,3584]{0,1:T(8,128)(2,1)} fusion(bf16[1024,3584]{1,0:T(8,128)(2,1)} %all-gather.4.cloned.1.call-done, bf16[1024,1024]{1,0:T(8,128)(2,1)S(1)} %copy-done), kind=kOutput, calls=%fused_computation.2 | convolution fusion | flops 7519862784 | bytes 16777216 | tf_op jit(solution)/shard_map/dot_general | solution.py:8
  258.7 0.0 reduce-scatter.6.cloned.1.call-update
  258.7 0.2 reduce-scatter.4.cloned.1.call-start
  258.9 11.3 %fusion.11 = f32[1024,1024]{1,0:T(8,128)S(1)} fusion(bf16[1024,3584]{1,0:T(8,128)(2,1)} %all-gather.4.cloned.1.call-done, bf16[1024,3584]{1,0:T(8,128)(2,1)} %param.10), kind=kOutput, calls=%fused_computation.20 | convolution fusion | flops 7516192768 | bytes 18874368 | tf_op jit(solution)/shard_map/dot_general | solution.py:40
  270.2 13.4 %add_convert_fusion = bf16[1024,1024]{1,0:T(8,128)(2,1)} fusion(f32[1024,1024]{1,0:T(8,128)S(1)} %fusion.11, bf16[1024,3584]{1,0:T(8,128)(2,1)} %all-gather.6.cloned.1.call-done, bf16[1024,3584]{1,0:T(8,128)(2,1)} %param.11), kind=kOutput, calls=%fused_computation.4 | convolution fusion | flops 7518289920 | bytes 20971520 | tf_op jit(solution)/shard_map/dot_general | solution.py:46
  283.6 0.0 reduce-scatter.4.cloned.1.call-update
  283.6 33.8 %reduce-scatter.8.cloned.1.call-done = bf16[256,3584]{0,1:T(8,128)(2,1)} async-done(((bf16[1024,3584]{0,1:T(8,128)(2,1)}), bf16[256,3584]{0,1:T(8,128)(2,1)}) %reduce-scatter.8.cloned.1.call-update) | async-done | bytes 1835024 | tf_op jit(solution)/shard_map/reduce_scatter | solution.py:36
  317.4 1.8 multiply_convert_fusion
  319.3 2.6 copy.10
  321.8 69.9 %reduce-scatter.6.cloned.1.call-done = bf16[256,3584]{0,1:T(8,128)(2,1)} async-done(((bf16[1024,3584]{0,1:T(8,128)(2,1)}), bf16[256,3584]{0,1:T(8,128)(2,1)}) %reduce-scatter.6.cloned.1.call-update) | async-done | bytes 1835024 | tf_op jit(solution)/shard_map/reduce_scatter | solution.py:33
  391.8 1.8 multiply_convert_fusion.1
  393.6 2.6 copy.9
  396.2 28.9 %reduce-scatter.4.cloned.1.call-done = bf16[256,1024]{1,0:T(8,128)(2,1)} async-done(((bf16[1024,1024]{1,0:T(8,128)(2,1)}), bf16[256,1024]{1,0:T(8,128)(2,1)}) %reduce-scatter.4.cloned.1.call-update) | async-done | bytes 524304 | tf_op jit(solution)/shard_map/reduce_scatter | solution.py:43
Async XLA Ops:
  7.2 36.5 %all-gather.8.cloned.1.call-start = ((), (), s32[]{:S(2)}) async-start(), calls=%async_computation.6 | async-start | bytes 2621440 | tf_op jit(solution)/shard_map/all_gather | solution.py:28
  7.9 137.7 %all-gather.6.cloned.1.call-start = ((), (), s32[]{:S(2)}) async-start(), calls=%async_computation.4 | async-start | bytes 8257536 | tf_op jit(solution)/shard_map/all_gather | solution.py:26
  11.9 233.8 %all-gather.4.cloned.1.call-start = ((), (), s32[]{:S(2)}) async-start(), calls=%async_computation.3 | async-start | bytes 8257536 | tf_op jit(solution)/shard_map/all_gather | solution.py:25
  12.6 304.8 %reduce-scatter.8.cloned.1.call-start = ((), (), s32[]{:S(2)}) async-start(), calls=%async_computation.8 | async-start | bytes 9175040 | tf_op jit(solution)/shard_map/reduce_scatter | solution.py:36
  158.3 87.4 %copy-start = (bf16[1024,1024]{1,0:T(8,128)(2,1)S(1)}, bf16[1024,1024]{1,0:T(8,128)(2,1)}, u32[]{:S(2)}) copy-start(bf16[1024,1024]{1,0:T(8,128)(2,1)} %all-gather.8.cloned.1.call-done) | copy-start | bytes 6291460
  158.3 233.5 %reduce-scatter.6.cloned.1.call-start = ((), (), s32[]{:S(2)}) async-start(), calls=%async_computation.7 | async-start | bytes 9175040 | tf_op jit(solution)/shard_map/reduce_scatter | solution.py:33
  258.7 166.4 %reduce-scatter.4.cloned.1.call-start = ((), (), s32[]{:S(2)}) async-start(), calls=%async_computation.5 | async-start | bytes 2621440 | tf_op jit(solution)/shard_map/reduce_scatter | solution.py:43
Sparse Core Ops, SparseCore 0:
  9.7 34.0 all-gather.7
  46.6 98.9 all-gather.5
  148.5 97.0 all-gather.3
  247.9 69.4 reduce-scatter.7
  319.7 72.0 reduce-scatter.5
  394.6 30.4 reduce-scatter.3
where the time goes:
time: 432 us
  waiting for transfers between devices  354 us (82%)
  matrix products  50.3 us (12%)
  between operations  14.1 us (3%)
  other arithmetic  7.6 us (2%)
  local copies, waits for them, and re-layouts  5.13 us (1%)
    all_gather x1, waiting for transfers between devices, body(): lax.all_gather(up_grad, 'row', axis=0, tiled=True)  102 us
    all_gather x1, waiting for transfers between devices, body(): lax.all_gather(gate_grad, 'row', axis=0, tiled=True)  87.3 us
    reduce_scatter x1, waiting for transfers between devices, body(): lax.psum_scatter(gate_partial.astype(jnp.bfloat16), 'dp', scatter_dimensi...  69.9 us
    reduce_scatter x1, waiting for transfers between devices, body(): lax.psum_scatter(up_partial.astype(jnp.bfloat16), 'dp', scatter_dimension...  33.8 us
    all_gather x1, waiting for transfers between devices, body(): group_input = lax.all_gather(layer_input, 'col', axis=0, tiled=True)  31.1 us
    reduce_scatter x1, waiting for transfers between devices, body(): lax.psum_scatter((partial_value + lax.dot_general(group_up, up_weight, ((...  28.9 us
    dot_general x2, matrix products, weight_term(): lax.dot_general(first_rows, second_rows, (((0,), (0,)), ((), ())), prefer...  25.7 us
    dot_general x1, matrix products, body(): lax.dot_general(group_up, up_weight, (((1,), (1,)), ((), ())), preferred_...  13.4 us
  transfers between devices with their start and end apart: 6, of which 6 were waited for; matrix products, arithmetic and copies ran while one was open for 15% of the time, Pallas kernels for 0%

commit v1 on v0

v1 whole, which is shorter than its diff:
```python
import jax
import jax.numpy as jnp
from jax import lax
from jax.experimental import pallas as pl
from jax.experimental.pallas import tpu as pltpu
from jax.sharding import PartitionSpec as P

CHUNKS = ((3072, 512, False), (0, 1024, True), (1024, 1024, False), (2048, 1024, False))
SAME_Z = [[0, 2, 4, 6], [1, 3, 5, 7]]
ROW_UP = [(i, (i + 2) % 8) for i in range(8)]
ROW_DOWN = [(i, (i - 2) % 8) for i in range(8)]
ROW_SWAP = [(i, i ^ 1) for i in range(8)]
COL_UP = [(i, (i + 1) % 4) for i in range(4)]
COL_DOWN = [(i, (i - 1) % 4) for i in range(4)]
COL_FAR = [(i, (i + 2) % 4) for i in range(4)]
CORE_SWAP = [(i, i ^ 1) for i in range(4)]
PAIR_SWAP = [(i, i ^ 2) for i in range(4)]


TILES = 2
VMEM_BYTES = 40 * 1024 * 1024
NO_COST = pl.CostEstimate(flops=0, bytes_accessed=0, transcendentals=0)


def after(value, *earlier):
    return lax.optimization_barrier((value, *earlier))[0]


def after_all(values, *earlier):
    return list(lax.optimization_barrier((*values, *earlier)))[: len(values)]


def params():
    return pltpu.CompilerParams(dimension_semantics=("arbitrary",), vmem_limit_bytes=VMEM_BYTES)


def gate_up_grads(hidden_grad, gate_pre, up_pre):
    gate_value = gate_pre.astype(jnp.float32)
    sigmoid_gate = jax.nn.sigmoid(gate_value)
    grad_value = hidden_grad.astype(jnp.float32)
    gate_grad = (
        grad_value
        * up_pre.astype(jnp.float32)
        * sigmoid_gate
        * (1.0 + gate_value * (1.0 - sigmoid_gate))
    ).astype(jnp.bfloat16)
    up_grad = (grad_value * gate_value * sigmoid_gate).astype(jnp.bfloat16)
    return jnp.concatenate([gate_grad, up_grad], axis=1)


def order_input(group_input, row, dp):
    tokens, width = group_input.shape
    half, quarter = tokens // 8, width // 4
    picks = (jnp.arange(8, dtype=jnp.int32) ^ (row % 2)).astype(jnp.int32)
    parts = (dp ^ jnp.array([3, 1, 2, 0], jnp.int32)).astype(jnp.int32)

    def kernel(picks_ref, parts_ref, in_ref, out_ref):
        for i in range(8):
            rows = pl.ds(pl.multiple_of(picks_ref[i] * half, half), half)
            for k in range(4):
                columns = pl.ds(pl.multiple_of(parts_ref[k] * quarter, quarter), quarter)
                out_ref[k * quarter : (k + 1) * quarter, i * half : (i + 1) * half] = in_ref[rows, columns].T

    return pl.pallas_call(
        kernel,
        out_shape=jax.ShapeDtypeStruct((width, tokens), group_input.dtype),
        grid_spec=pltpu.PrefetchScalarGridSpec(
            num_scalar_prefetch=2,
            grid=(1,),
            in_specs=[pl.BlockSpec((tokens, width), lambda i, *_: (0, 0))],
            out_specs=pl.BlockSpec((width, tokens), lambda i, *_: (0, 0)),
        ),
        compiler_params=params(),
        cost_estimate=NO_COST,
        name="order_input",
    )(picks, parts, group_input)


def join_rows(places, pieces):
    rows, columns = pieces[0].shape
    count = len(pieces)

    def kernel(places_ref, *refs):
        out_ref, sems = refs[count], refs[count + 1]
        copies = []
        for k in range(count):
            at = pl.ds(pl.multiple_of(places_ref[k] * rows, rows), rows)
            copies.append(pltpu.make_async_copy(refs[k], out_ref.at[at, :], sems.at[k]))
        for copy in copies:
            copy.start()
        for copy in copies:
            copy.wait()

    return pl.pallas_call(
        kernel,
        out_shape=jax.ShapeDtypeStruct((rows * count, columns), pieces[0].dtype),
        grid_spec=pltpu.PrefetchScalarGridSpec(
            num_scalar_prefetch=1,
            grid=(1,),
            in_specs=[pl.BlockSpec(memory_space=pl.ANY)] * count,
            out_specs=pl.BlockSpec((rows * count, columns), lambda i, places: (0, 0)),
            scratch_shapes=[pltpu.SemaphoreType.DMA((count,))],
        ),
        compiler_params=params(),
        cost_estimate=NO_COST,
        name="join_rows",
    )(places, *pieces)


def chunk_grads(places, pieces, input_columns, gate_weight, up_weight, start, total, last):
    count = len(pieces)
    rows, hidden = pieces[0].shape
    tokens = rows * count
    width = (input_columns if gate_weight is None else gate_weight).shape[0]
    w = hidden // 2
    tile = width // TILES
    half = TILES // 2
    column = start // w
    block = tokens // 4
    with_weight, with_input = input_columns is not None, gate_weight is not None

    def kernel(places_ref, *refs):
        refs = list(refs)
        take = lambda k: [refs.pop(0) for _ in range(k)]
        piece_refs = take(count)
        input_refs = take(1) if with_weight else []
        weight_refs = take(2) if with_input else []
        total_refs = take(1) if total is not None else []
        part_refs = take(2) if with_weight else []
        sum_refs = take(4 if last else 1) if with_input else []
        if count > 1:
            rows_ref = refs.pop(0)

            @pl.when(pl.program_id(0) == 0)
            def _():
                for k in range(count):
                    rows_ref[pl.ds(pl.multiple_of(places_ref[k] * rows, rows), rows), :] = piece_refs[k][...]
        else:
            rows_ref = piece_refs[0]

        if with_weight:
            part = jnp.dot(input_refs[0][...], rows_ref[...], preferred_element_type=jnp.float32).astype(jnp.bfloat16)

            @pl.when(pl.program_id(0) < half)
            def _():
                part_refs[0][...] = part

            @pl.when(pl.program_id(0) >= half)
            def _():
                part_refs[1][...] = part

        if with_input:
            across = (((1,), (1,)), ((), ()))
            term = lax.dot_general(rows_ref[:, :w], weight_refs[0][...], across, preferred_element_type=jnp.float32)
            term += lax.dot_general(rows_ref[:, w:], weight_refs[1][...], across, preferred_element_type=jnp.float32)
            if total_refs:
                term += total_refs[0][...]
            if last:
                sum_ref = refs.pop(0)
                sum_ref[...] = term
                for k in range(4):
                    at = pl.multiple_of(places_ref[8 + k] * block, block)
                    sum_refs[k][...] = sum_ref[pl.ds(at, block), :].astype(jnp.bfloat16)
            else:
                sum_refs[0][...] = term

    in_specs = [pl.BlockSpec((rows, hidden), lambda i, _: (0, 0), pipeline_mode=pl.Buffered(1))] * count
    operands = [*pieces]
    out_shape, out_specs, scratch = [], [], []
    if count > 1:
        scratch.append(pltpu.VMEM((tokens, hidden), jnp.bfloat16))
    if with_weight:
        in_specs.append(pl.BlockSpec((tile, tokens), lambda i, _: (i, 0)))
        operands.append(input_columns)
        out_shape += [jax.ShapeDtypeStruct((width // 2, hidden), jnp.bfloat16)] * 2
        out_specs += [
            pl.BlockSpec((tile, hidden), lambda i, _: (jnp.minimum(i, half - 1), 0)),
            pl.BlockSpec((tile, hidden), lambda i, _: (jnp.maximum(i - half, 0), 0)),
        ]
    if with_input:
        in_specs += [pl.BlockSpec((tile, w), lambda i, _: (i, column))] * 2
        operands += [gate_weight, up_weight]
        if total is not None:
            in_specs.append(pl.BlockSpec((tokens, tile), lambda i, _: (0, i)))
            operands.append(total)
        if last:
            out_shape += [jax.ShapeDtypeStruct((block, width), jnp.bfloat16)] * 4
            out_specs += [pl.BlockSpec((block, tile), lambda i, _: (0, i))] * 4
            scratch.append(pltpu.VMEM((tokens, tile), jnp.float32))
        else:
            out_shape.append(jax.ShapeDtypeStruct((tokens, width), jnp.float32))
            out_specs.append(pl.BlockSpec((tokens, tile), lambda i, _: (0, i)))
    return pl.pallas_call(
        kernel,
        out_shape=tuple(out_shape),
        grid_spec=pltpu.PrefetchScalarGridSpec(
            num_scalar_prefetch=1, grid=(TILES,), in_specs=in_specs, out_specs=tuple(out_specs), scratch_shapes=scratch
        ),
        compiler_params=params(),
        cost_estimate=NO_COST,
        name="chunk_grads",
    )(places, *operands)


def body(layer_input, hidden_grad, gate_pre, up_pre, gate_weight, up_weight):
    row, col, dp = lax.axis_index("row"), lax.axis_index("col"), lax.axis_index("dp")
    y, z_hi = row // 2, row % 2
    tokens, width = layer_input.shape
    quarter = width // 4
    count = len(CHUNKS)
    steps = jnp.arange(4, dtype=jnp.int32)
    blocks = (y + steps) % 4
    places = jnp.concatenate([jnp.stack([2 * blocks, 2 * blocks + 1], axis=1).reshape(8), (col + steps) % 4])
    places = places.astype(jnp.int32)

    swap = lambda value: lax.ppermute(value, "row", ROW_SWAP)
    up = lambda value: lax.ppermute(value, "row", ROW_UP)
    down = lambda value: lax.ppermute(value, "row", ROW_DOWN)
    gather = lambda value: lax.all_gather(value, "row", axis=0, tiled=True, axis_index_groups=SAME_Z)
    own, other, below, above, other_below, other_above, far, other_far, rows = ([None] * count for _ in range(9))

    def grads_of(c):
        s, w, _ = CHUNKS[c]
        return gate_up_grads(*(a[:, s : s + w] for a in (hidden_grad, gate_pre, up_pre)))

    group_input = lax.all_gather(layer_input, "col", axis=0, tiled=True)
    own[0] = grads_of(0)
    other[0] = swap(own[0])
    below[0], above[0] = up(own[0]), down(own[0])
    hidden_grad = after(hidden_grad, own[0])
    for c in range(1, count):
        own[c] = grads_of(c)
    below[2], above[2] = up(own[2]), down(own[2])
    first = (below[0], above[0], other[0])
    other[1] = swap(after(own[1], *first))
    other_0 = after(other[0], *first)
    other_below[0], other_above[0] = up(other_0), down(other_0)
    far[0] = up(after(below[0], *first))
    other[2] = swap(after(own[2], below[2]))
    other[3] = swap(after(own[3], other[1]))
    second = (below[2], above[2], other_below[0], other_above[0])
    other_far[0] = down(after(other_above[0], *second))
    far[2] = up(after(below[2], *second))
    whole_1 = join_rows(steps[:2], after_all([own[1], other[1]], *second))
    rows[1] = gather(whole_1)
    third = (far[0], other_far[0], other[2])
    input_columns = order_input(after(group_input, *third, whole_1), row, dp)
    other_below[2], other_above[2] = up(other[2]), down(other[2])
    own_3 = after(own[3], other_below[2], other_above[2])
    below[3], above[3] = up(own_3), down(own_3)
    before = [third, (other_below[2], other_above[2]), (), ()]

    inverse_groups = 1.0 / lax.axis_size("dp")
    gate_out = jnp.zeros((quarter, gate_weight.shape[1]), jnp.bfloat16)
    up_out = jnp.zeros((quarter, gate_weight.shape[1]), jnp.bfloat16)
    total = None
    chip_send, pair_parts = [None] * count, [None] * count
    for c, (s, w, gathered) in enumerate(CHUNKS):
        earlier = [*before[c]]
        if c >= 1:
            earlier += [pair_parts[c - 1], total]
        if c == 1:
            other_far[2] = down(after(other_above[2], chip_send[0]))
            other_3 = after(other[3], below[3], other_far[2])
            other_below[3], other_above[3] = up(other_3), down(other_3)
            far[3], other_far[3] = up(below[3]), down(other_above[3])
            before[2:] = [(above[3], other_below[3], other_above[3]), (far[3], other_far[3])]
        pieces = [rows[c]] if gathered else [
            own[c], other[c], above[c], other_above[c], far[c], other_far[c], below[c], other_below[c]
        ]
        if c == count - 1:
            shares = chunk_grads(
                places, after_all(pieces, chip_send[c - 1], total), None, gate_weight, up_weight, s, total, True
            )
            mine, next_one, across, last_one = shares
            shares = (
                mine,
                lax.ppermute(next_one, "col", COL_UP),
                lax.ppermute(last_one, "col", COL_DOWN),
                lax.ppermute(across, "col", COL_FAR),
            )
            earlier += shares[:1]
        pieces = after_all(pieces, *earlier)
        send, keep = chunk_grads(places, pieces, input_columns, None, None, s, None, False)
        core_part = lax.ppermute(send, "dp", CORE_SWAP)
        chip_send[c] = (keep[:quarter].astype(jnp.float32) + core_part[:quarter].astype(jnp.float32)).astype(jnp.bfloat16)
        pair_part = pair_parts[c] = lax.ppermute(chip_send[c], "dp", PAIR_SWAP)
        if c < count - 1:
            pieces = after_all(pieces, chip_send[c])
            (total,) = chunk_grads(places, pieces, None, gate_weight, up_weight, s, total, False)

        def finish(columns):
            value = keep[quarter:, columns].astype(jnp.float32) + core_part[quarter:, columns].astype(jnp.float32)
            return ((value + pair_part[:, columns].astype(jnp.float32)) * inverse_groups).astype(jnp.bfloat16)

        gate_out = lax.dynamic_update_slice(gate_out, finish(slice(0, w)), (0, s))
        up_out = lax.dynamic_update_slice(up_out, finish(slice(w, 2 * w)), (0, s))

    input_grad = sum(share.astype(jnp.float32) for share in shares)
    halves = input_grad.reshape(2, tokens // 2, width)
    input_grad = jnp.where(z_hi == 0, halves, halves[::-1]).reshape(tokens, width).astype(jnp.bfloat16)
    return input_grad, gate_out, up_out


def solution(mesh):
    return jax.shard_map(
        body,
        mesh=mesh,
        in_specs=(
            P(("dp", "col"), "row"),
            P(("dp", "row"), "col"),
            P(("dp", "row"), "col"),
            P(("dp", "row"), "col"),
            P("row", "col"),
            P("row", "col"),
        ),
        out_specs=(P(("dp", "col"), "row"), P(("row", "dp"), "col"), P(("row", "dp"), "col")),
        check_vma=False,
    )
```

time: 432 us -> 250 us (0.58)
  waiting for transfers between devices: 354 us -> 92.7 us
  Pallas kernels: 0 us -> 51.9 us
  matrix products: 50.3 us -> 0 us
  starting transfers between devices: 0.42 us -> 44.8 us
  local copies, waits for them, and re-layouts: 5.13 us -> 30.1 us
  other arithmetic: 7.6 us -> 14.7 us
    all_gather x2 -> x1, waiting for transfers between devices: 189 us -> 10.6 us  [body(): lax.all_gather(value, 'row', axis=0, tiled=True, axis_index_groups=SAME_Z)]
    reduce_scatter x3 -> x0, waiting for transfers between devices: 133 us -> none  [the longest x1 69.9 us: body(): lax.psum_scatter(gate_partial.astype(jnp.bfloat16), 'dp', scatter_dimensi...]
    ppermute x0 -> x33, waiting for transfers between devices: none -> 81.4 us  [the longest x9 33 us: body(): down = lambda value: lax.ppermute(value, 'row', ROW_DOWN)]
    pallas_call x0 -> x10, Pallas kernels: none -> 51.9 us  [the longest x8 49.1 us: chunk_grads(): pl.pallas_call(kernel, out_shape=tuple(out_shape), grid_spec=pltpu.Prefet...]
    dot_general x4 -> x0, matrix products: 50.3 us -> none  [the longest x2 25.7 us: weight_term(): lax.dot_general(first_rows, second_rows, (((0,), (0,)), ((), ())), prefer...]
    ppermute x0 -> x33, starting transfers between devices: none -> 44.7 us  [the longest x9 17.1 us: body(): down = lambda value: lax.ppermute(value, 'row', ROW_DOWN)]
    all_gather x1, waiting for transfers between devices: 31.1 us -> 0.01 us  [body(): group_input = lax.all_gather(layer_input, 'col', axis=0, tiled=True)]
    unnamed x4 -> x136, local copies, waits for them, and re-layouts: 5.13 us -> 29.8 us
  transfers between devices with their start and end apart: 6 -> 35, of which waited for: 6 -> 17; matrix products, arithmetic and copies ran while one was open for 15% -> 6% of each run, Pallas kernels for 0% -> 13%
where the time goes in v1:
time: 250 us; the launch traced here: 249 us
  waiting for transfers between devices  92.7 us (37%)
  Pallas kernels  51.9 us (21%)
  starting transfers between devices  44.8 us (18%)
  local copies, waits for them, and re-layouts  30.1 us (12%)
  other arithmetic  14.7 us (6%)
  between operations  14.6 us (6%)
    pallas_call x8, Pallas kernels, chunk_grads(): pl.pallas_call(kernel, out_shape=tuple(out_shape), grid_spec=pltpu.Prefet...  49.1 us
    ppermute x9, waiting for transfers between devices, body(): down = lambda value: lax.ppermute(value, 'row', ROW_DOWN)  33 us
    unnamed x136, local copies, waits for them, and re-layouts  29.8 us
    ppermute x9, starting transfers between devices, body(): down = lambda value: lax.ppermute(value, 'row', ROW_DOWN)  17.1 us
    ppermute x9, waiting for transfers between devices, body(): up = lambda value: lax.ppermute(value, 'row', ROW_UP)  14.6 us
    ppermute x1, waiting for transfers between devices, body(): lax.ppermute(across, 'col', COL_FAR)  12.1 us
    ppermute x4, waiting for transfers between devices, body(): swap = lambda value: lax.ppermute(value, 'row', ROW_SWAP)  10.9 us
    all_gather x1, waiting for transfers between devices, body(): lax.all_gather(value, 'row', axis=0, tiled=True, axis_index_groups=SAME_Z)  10.6 us
  transfers between devices with their start and end apart: 35, of which 17 were waited for; matrix products, arithmetic and copies ran while one was open for 6% of the time, Pallas kernels for 13%

profile of v1, /device:TPU:1, one launch (start us, length us, event | category | flops | bytes accessed | tf_op | source)
XLA Modules:
  0.0 248.8 jit_solution(17081216634084997502)
XLA Ops:
  9.2 2.2 collective-permute-start
  11.3 1.5 collective-permute-start.1
  12.9 3.6 %collective-permute-start.2 = (bf16[128,1024]{1,0:T(8,128)(2,1)S(1)}, bf16[128,1024]{1,0:T(8,128)(2,1)S(1)}, u32[]{:S(2)}, u32[]{:S(2)}) collective-permute-start(bf16[128,1024]{1,0:T(8,128)(2,1)S(1)} %pad_maximum_fusion.3.refs_0_), channel_id=1, source_target_pairs={{0,4},{4,0},{8,12},{12,8},{16,20},{20,16},{24,28},{28,24},{1,5},{5... | collective-permute-start | bytes 786440 | tf_op jit(solution)/shard_map/ppermute | solution.py:216
  16.5 3.2 %fusion.9 = (bf16[128,1024]{1,0:T(8,128)(2,1)S(1)}, bf16[128,1024]{1,0:T(8,128)(2,1)}, bf16[128,1024]{1,0:T(8,128)(2,1)S(1)}, bf16[128,1024]{1,0:T(8,128)(2,1)},...) fusion(bf16[128,3584]{1,0:T(8,128)(2,1)} %param.10, bf16[128,3584]{1,0:T(8,128)(2,1)} %param.9, ...), kind=kLoop, calls=%fused_computation.33 | loop fusion | flops 6291456 | bytes 3932160 | tf_op jit(solution)/shard_map/convert_element_type | solution.py:46
  19.8 2.7 %collective-permute-start.13 = (bf16[128,2048]{1,0:T(8,128)(2,1)S(1)}, bf16[128,2048]{1,0:T(8,128)(2,1)S(1)}, u32[]{:S(2)}, u32[]{:S(2)}) collective-permute-start(bf16[128,2048]{1,0:T(8,128)(2,1)S(1)} %pad_maximum_fusion.2.refs_0_), channel_id=1, source_target_pairs={{0,24},{4,28},{8,0},{12,4},{16,8},{20,12},{24,16},{28,20},{1,25},{... | collective-permute-start | bytes 1572872 | tf_op jit(solution)/shard_map/ppermute | solution.py:218
  23.2 1.4 collective-permute-start.3
  26.8 10.8 %collective-permute-done.11.refs_3_ = bf16[128,1024]{1,0:T(8,128)(2,1)S(1)} collective-permute-done((bf16[128,1024]{1,0:T(8,128)(2,1)S(1)}, bf16[128,1024]{1,0:T(8,128)(2,1)S(1)}, u32[]{:S(2)}, u32[]{:S(2)}) %collective-permute-start.11) | collective-permute-done | bytes 262176 | tf_op jit(solution)/shard_map/ppermute | solution.py:218
  40.3 1.6 join_rows.1
  44.5 1.4 collective-permute-start.15
  46.7 2.6 %collective-permute-done.12.refs_4_ = bf16[128,1024]{1,0:T(8,128)(2,1)S(1)} collective-permute-done((bf16[128,1024]{1,0:T(8,128)(2,1)S(1)}, bf16[128,1024]{1,0:T(8,128)(2,1)S(1)}, u32[]{:S(2)}, u32[]{:S(2)}) %collective-permute-start.12) | collective-permute-done | bytes 262176 | tf_op jit(solution)/shard_map/ppermute | solution.py:217
  50.9 4.0 %collective-permute-done.6.refs_1_ = bf16[128,2048]{1,0:T(8,128)(2,1)S(1)} collective-permute-done((bf16[128,2048]{1,0:T(8,128)(2,1)S(1)}, bf16[128,2048]{1,0:T(8,128)(2,1)S(1)}, u32[]{:S(2)}, u32[]{:S(2)}) %collective-permute-start.6) | collective-permute-done | bytes 524320 | tf_op jit(solution)/shard_map/ppermute | solution.py:216
  55.7 1.8 copy-done.27
  59.1 3.4 %chunk_grads.8 = (bf16[512,1024]{1,0:T(8,128)(2,1)S(1)}, bf16[512,1024]{1,0:T(8,128)(2,1)S(1)}) custom-call(s32[12]{0:T(128)S(1)} %pad_add_fusion.1.places_ref, bf16[128,1024]{1,0:T(8,128)(2,1)S(1)} %pad_maximum_fusion.3.refs_0_, bf16[128,1024]{1,0:T(8,128)(2,1)S(1)} %copy-done.39, bf16[128,1024]{1,0:T(8,128)(2,1)S(1)} %copy-done.37, ...), custom_call_target="tpu_custom_call" | custom-call | tf_op jit(solution)/shard_map/chunk_grads/pallas_call | solution.py:193
  62.5 2.9 %collective-permute-start.16 = (bf16[512,1024]{1,0:T(8,128)(2,1)S(1)}, bf16[512,1024]{1,0:T(8,128)(2,1)S(1)}, u32[]{:S(2)}, u32[]{:S(2)}) collective-permute-start(bf16[512,1024]{1,0:T(8,128)(2,1)S(1)} %get-tuple-element.99), channel_id=1, source_target_pairs={{0,32},{32,0},{64,96},{96,64},{1,33},{33,1},{65,97},{97,65},{2,34}... | collective-permute-start | bytes 3145736 | tf_op jit(solution)/shard_map/ppermute | solution.py:285
  65.4 2.5 collective-permute-start.8
  69.2 3.2 %copy-done = bf16[1024,3584]{1,0:T(8,128)(2,1)S(1)} copy-done((bf16[1024,3584]{1,0:T(8,128)(2,1)S(1)}, bf16[1024,3584]{1,0:T(8,128)(2,1)}, u32[]{:S(2)}) %copy-start) | copy-done | bytes 7340056
  72.3 4.6 %chunk_grads.9.refs_3_ = f32[1024,1024]{1,0:T(8,128)S(1)} custom-call(s32[12]{0:T(128)S(1)} %pad_add_fusion.1.places_ref, bf16[128,1024]{1,0:T(8,128)(2,1)S(1)} %pad_maximum_fusion.3.refs_0_, bf16[128,1024]{1,0:T(8,128)(2,1)S(1)} %copy-done.39, bf16[128,1024]{1,0:T(8,128)(2,1)S(1)} %copy-done.37, bf16[128,1024]{1,0:T(8,128)(2,1)S(1)} %copy-done.41, ...), custom_call_target="tpu_custom_call" | custom-call | tf_op jit(solution)/shard_map/chunk_grads/pallas_call | solution.py:193
  77.0 2.0 copy-done.3
  79.0 11.6 %collective-permute-done.8.refs_3_ = bf16[128,2048]{1,0:T(8,128)(2,1)S(1)} collective-permute-done((bf16[128,2048]{1,0:T(8,128)(2,1)S(1)}, bf16[128,2048]{1,0:T(8,128)(2,1)S(1)}, u32[]{:S(2)}, u32[]{:S(2)}) %collective-permute-start.8) | collective-permute-done | bytes 524320 | tf_op jit(solution)/shard_map/ppermute | solution.py:218
  90.6 3.4 %collective-permute-done.7.refs_7_ = bf16[128,2048]{1,0:T(8,128)(2,1)S(1)} collective-permute-done((bf16[128,2048]{1,0:T(8,128)(2,1)S(1)}, bf16[128,2048]{1,0:T(8,128)(2,1)S(1)}, u32[]{:S(2)}, u32[]{:S(2)}) %collective-permute-start.7) | collective-permute-done | bytes 524320 | tf_op jit(solution)/shard_map/ppermute | solution.py:217
  94.8 10.6 %all-gather.5.cloned.1.call-done.refs_0_ = bf16[1024,2048]{1,0:T(8,128)(2,1)} async-done(((bf16[256,2048]{1,0:T(8,128)(2,1)}), bf16[1024,2048]{1,0:T(8,128)(2,1)}) %all-gather.5.cloned.1.call-update) | async-done | bytes 4194320 | tf_op jit(solution)/shard_map/all_gather | solution.py:219
  105.5 2.2 copy-done.1
  107.7 5.7 %chunk_grads.10 = (bf16[512,2048]{1,0:T(8,128)(2,1)S(1)}, bf16[512,2048]{1,0:T(8,128)(2,1)S(1)}) custom-call(s32[12]{0:T(128)S(1)} %pad_add_fusion.1.places_ref, bf16[1024,2048]{1,0:T(8,128)(2,1)S(1)} %copy-done.1, bf16[1024,1024]{1,0:T(8,128)(2,1)S(1)} %order_input.1.refs_8_.refs_1_), custom_call_target="tpu_custom_call" | custom-call | tf_op jit(solution)/shard_map/chunk_grads/pallas_call | solution.py:193
  115.4 2.9 %collective-permute-start.4 = (bf16[128,2048]{1,0:T(8,128)(2,1)S(1)}, bf16[128,2048]{1,0:T(8,128)(2,1)S(1)}, u32[]{:S(2)}, u32[]{:S(2)}) collective-permute-start(bf16[128,2048]{1,0:T(8,128)(2,1)S(1)} %pad_maximum_fusion.refs_0_), channel_id=1, source_target_pairs={{0,4},{4,0},{8,12},{12,8},{16,20},{20,16},{24,28},{28,24},{1,5},{5... | collective-permute-start | bytes 1572872 | tf_op jit(solution)/shard_map/ppermute | solution.py:216
  118.9 2.1 collective-permute-start.17
  121.0 1.7 add_convert_fusion.2
  123.2 6.9 %collective-permute-done.4.refs_1_ = bf16[128,2048]{1,0:T(8,128)(2,1)S(1)} collective-permute-done((bf16[128,2048]{1,0:T(8,128)(2,1)S(1)}, bf16[128,2048]{1,0:T(8,128)(2,1)S(1)}, u32[]{:S(2)}, u32[]{:S(2)}) %collective-permute-start.4) | collective-permute-done | bytes 524320 | tf_op jit(solution)/shard_map/ppermute | solution.py:216
  131.0 1.4 collective-permute-done.10.refs_6_
  132.3 2.4 collective-permute-start.18
  134.7 7.2 %chunk_grads.11.refs_10_ = f32[1024,1024]{1,0:T(8,128)S(1)} custom-call(s32[12]{0:T(128)S(1)} %pad_add_fusion.1.places_ref, bf16[1024,2048]{1,0:T(8,128)(2,1)S(1)} %copy-done.2, bf16[1024,3584]{1,0:T(8,128)(2,1)} %refs_8_.5, bf16[1024,3584]{1,0:T(8,128)(2,1)} %refs_9_.5, f32[1024,1024]{1,0:T(8,128)S(1)} %copy-done.4), custom_call_target="tpu_custom_call" | custom-call | tf_op jit(solution)/shard_map/chunk_grads/pallas_call | solution.py:193
  141.9 1.7 collective-permute-done.22.refs_4_
  143.6 10.4 %collective-permute-done.18.refs_3_ = bf16[128,2048]{1,0:T(8,128)(2,1)S(1)} collective-permute-done((bf16[128,2048]{1,0:T(8,128)(2,1)S(1)}, bf16[128,2048]{1,0:T(8,128)(2,1)S(1)}, u32[]{:S(2)}, u32[]{:S(2)}) %collective-permute-start.18) | collective-permute-done | bytes 524320 | tf_op jit(solution)/shard_map/ppermute | solution.py:218
  155.6 5.9 %chunk_grads.12 = (bf16[512,2048]{1,0:T(8,128)(2,1)S(1)}, bf16[512,2048]{1,0:T(8,128)(2,1)S(1)}) custom-call(s32[12]{0:T(128)S(1)} %pad_add_fusion.1.places_ref, bf16[128,2048]{1,0:T(8,128)(2,1)S(1)} %pad_maximum_fusion.2.refs_0_, bf16[128,2048]{1,0:T(8,128)(2,1)S(1)} %copy-done.9, bf16[128,2048]{1,0:T(8,128)(2,1)S(1)} %copy-done.6, ...), custom_call_target="tpu_custom_call" | custom-call | tf_op jit(solution)/shard_map/chunk_grads/pallas_call | solution.py:193
  162.4 1.6 collective-permute-start.26
  164.0 3.8 %collective-permute-done.26 = bf16[512,2048]{1,0:T(8,128)(2,1)S(1)} collective-permute-done((bf16[512,2048]{1,0:T(8,128)(2,1)S(1)}, bf16[512,2048]{1,0:T(8,128)(2,1)S(1)}, u32[]{:S(2)}, u32[]{:S(2)}) %collective-permute-start.26) | collective-permute-done | bytes 2097184 | tf_op jit(solution)/shard_map/ppermute | solution.py:285
  169.5 2.4 collective-permute-start.20
  171.9 7.4 %chunk_grads.13.refs_10_ = f32[1024,1024]{1,0:T(8,128)S(1)} custom-call(s32[12]{0:T(128)S(1)} %pad_add_fusion.1.places_ref, bf16[128,2048]{1,0:T(8,128)(2,1)S(1)} %pad_maximum_fusion.2.refs_0_, bf16[128,2048]{1,0:T(8,128)(2,1)S(1)} %copy-done.9, bf16[128,2048]{1,0:T(8,128)(2,1)S(1)} %copy-done.6, bf16[128,2048]{1,0:T(8,128)(2,1)S(1)} %copy-done.12, ...), custom_call_target="tpu_custom_call" | custom-call | tf_op jit(solution)/shard_map/chunk_grads/pallas_call | solution.py:193
  179.3 3.6 %collective-permute-done.19.refs_4_ = bf16[128,2048]{1,0:T(8,128)(2,1)S(1)} collective-permute-done((bf16[128,2048]{1,0:T(8,128)(2,1)S(1)}, bf16[128,2048]{1,0:T(8,128)(2,1)S(1)}, u32[]{:S(2)}, u32[]{:S(2)}) %collective-permute-start.19) | collective-permute-done | bytes 524320 | tf_op jit(solution)/shard_map/ppermute | solution.py:217
  183.0 7.5 %chunk_grads.14 = (bf16[256,1024]{1,0:T(8,128)(2,1)S(1)}, bf16[256,1024]{1,0:T(8,128)(2,1)S(1)}, bf16[256,1024]{1,0:T(8,128)(2,1)S(1)}, bf16[256,1024]{1,0:T(8,128)(2,1)S(1)}) custom-call(s32[12]{0:T(128)S(1)} %pad_add_fusion.1.places_ref, bf16[128,2048]{1,0:T(8,128)(2,1)S(1)} %pad_maximum_fusion.refs_0_, ...), custom_call_target="tpu_custom_call" | custom-call | tf_op jit(solution)/shard_map/chunk_grads/pallas_call | solution.py:193
  197.8 7.3 %chunk_grads.15 = (bf16[512,2048]{1,0:T(8,128)(2,1)}, bf16[512,2048]{1,0:T(8,128)(2,1)S(1)}) custom-call(s32[12]{0:T(128)S(1)} %pad_add_fusion.1.places_ref, bf16[128,2048]{1,0:T(8,128)(2,1)S(1)} %pad_maximum_fusion.refs_0_, bf16[128,2048]{1,0:T(8,128)(2,1)S(1)} %collective-permute-done.4.refs_1_, bf16[128,2048]{1,0:T(8,128)(2,1)S(1)} %copy-done.18, ...), custom_call_target="tpu_custom_call" | custom-call | tf_op jit(solution)/shard_map/chunk_grads/pallas_call | solution.py:193
  205.1 1.4 copy-done.32
  206.5 1.5 collective-permute-start.31
  208.0 1.6 multiply_convert_fusion.6
  211.8 1.5 collective-permute-start.28
  213.3 1.5 collective-permute-start.29
  216.5 2.0 fusion.31
  218.5 6.9 %collective-permute-done.27 = bf16[256,1024]{1,0:T(8,128)(2,1)S(1)} collective-permute-done((bf16[256,1024]{1,0:T(8,128)(2,1)S(1)}, bf16[256,1024]{1,0:T(8,128)(2,1)S(1)}, u32[]{:S(2)}, u32[]{:S(2)}) %collective-permute-start.27) | collective-permute-done | bytes 524320 | tf_op jit(solution)/shard_map/ppermute | solution.py:278
  225.4 12.1 %collective-permute-done.29 = bf16[256,1024]{1,0:T(8,128)(2,1)S(1)} collective-permute-done((bf16[256,1024]{1,0:T(8,128)(2,1)S(1)}, bf16[256,1024]{1,0:T(8,128)(2,1)S(1)}, u32[]{:S(2)}, u32[]{:S(2)}) %collective-permute-start.29) | collective-permute-done | bytes 524320 | tf_op jit(solution)/shard_map/ppermute | solution.py:280
  (196 shorter events, 40.4 us)
Async XLA Ops:
  7.2 48.5 %all-gather.3.cloned.1.call-start = ((), (), s32[]{:S(2)}) async-start(), calls=%async_computation | async-start | bytes 2621440 | tf_op jit(solution)/shard_map/all_gather | solution.py:226
  7.9 97.6 %all-gather.5.cloned.1.call-start = ((), (), s32[]{:S(2)}) async-start(), calls=%async_computation.1 | async-start | bytes 5242880 | tf_op jit(solution)/shard_map/all_gather | solution.py:219
  9.2 13.4 %collective-permute-start = (bf16[128,1024]{1,0:T(8,128)(2,1)S(1)}, bf16[128,1024]{1,0:T(8,128)(2,1)S(1)}, u32[]{:S(2)}, u32[]{:S(2)}) collective-permute-start(bf16[128,1024]{1,0:T(8,128)(2,1)S(1)} %pad_maximum_fusion.3.refs_0_), channel_id=1, source_target_pairs={{0,8},{4,12},{8,16},{12,20},{16,24},{20,28},{24,0},{28,4},{1,9},{5... | collective-permute-start | bytes 786440 | tf_op jit(solution)/shard_map/ppermute | solution.py:217
  11.3 11.2 %collective-permute-start.1 = (bf16[128,1024]{1,0:T(8,128)(2,1)S(1)}, bf16[128,1024]{1,0:T(8,128)(2,1)S(1)}, u32[]{:S(2)}, u32[]{:S(2)}) collective-permute-start(bf16[128,1024]{1,0:T(8,128)(2,1)S(1)} %pad_maximum_fusion.3.refs_0_), channel_id=1, source_target_pairs={{0,24},{4,28},{8,0},{12,4},{16,8},{20,12},{24,16},{28,20},{1,25},{... | collective-permute-start | bytes 786440 | tf_op jit(solution)/shard_map/ppermute | solution.py:218
  12.9 10.4 %collective-permute-start.2 = (bf16[128,1024]{1,0:T(8,128)(2,1)S(1)}, bf16[128,1024]{1,0:T(8,128)(2,1)S(1)}, u32[]{:S(2)}, u32[]{:S(2)}) collective-permute-start(bf16[128,1024]{1,0:T(8,128)(2,1)S(1)} %pad_maximum_fusion.3.refs_0_), channel_id=1, source_target_pairs={{0,4},{4,0},{8,12},{12,8},{16,20},{20,16},{24,28},{28,24},{1,5},{5... | collective-permute-start | bytes 786440 | tf_op jit(solution)/shard_map/ppermute | solution.py:216
  19.7 19.8 %collective-permute-start.5 = (bf16[128,2048]{1,0:T(8,128)(2,1)S(1)}, bf16[128,2048]{1,0:T(8,128)(2,1)S(1)}, u32[]{:S(2)}, u32[]{:S(2)}) collective-permute-start(bf16[128,2048]{1,0:T(8,128)(2,1)S(1)} %pad_maximum_fusion.2.refs_0_), channel_id=1, source_target_pairs={{0,8},{4,12},{8,16},{12,20},{16,24},{20,28},{24,0},{28,4},{1,9},{5... | collective-permute-start | bytes 1572872 | tf_op jit(solution)/shard_map/ppermute | solution.py:217
  19.8 19.7 %collective-permute-start.13 = (bf16[128,2048]{1,0:T(8,128)(2,1)S(1)}, bf16[128,2048]{1,0:T(8,128)(2,1)S(1)}, u32[]{:S(2)}, u32[]{:S(2)}) collective-permute-start(bf16[128,2048]{1,0:T(8,128)(2,1)S(1)} %pad_maximum_fusion.2.refs_0_), channel_id=1, source_target_pairs={{0,24},{4,28},{8,0},{12,4},{16,8},{20,12},{24,16},{28,20},{1,25},{... | collective-permute-start | bytes 1572872 | tf_op jit(solution)/shard_map/ppermute | solution.py:218
  22.5 24.2 %copy-start.67 = (s32[4]{0:T(128)S(1)}, s32[4]{0:T(128)}, u32[]{:S(2)}) copy-start(s32[4]{0:T(128)} %constant.76.clone) | copy-start | bytes 52
  23.2 17.1 %collective-permute-start.3 = (bf16[128,2048]{1,0:T(8,128)(2,1)S(1)}, bf16[128,2048]{1,0:T(8,128)(2,1)S(1)}, u32[]{:S(2)}, u32[]{:S(2)}) collective-permute-start(bf16[128,2048]{1,0:T(8,128)(2,1)S(1)} %pad_maximum_fusion.1.refs_0_), channel_id=1, source_target_pairs={{0,4},{4,0},{8,12},{12,8},{16,20},{20,16},{24,28},{28,24},{1,5},{5... | collective-permute-start | bytes 1572872 | tf_op jit(solution)/shard_map/ppermute | solution.py:216
  24.7 13.0 %collective-permute-start.11 = (bf16[128,1024]{1,0:T(8,128)(2,1)S(1)}, bf16[128,1024]{1,0:T(8,128)(2,1)S(1)}, u32[]{:S(2)}, u32[]{:S(2)}) collective-permute-start(bf16[128,1024]{1,0:T(8,128)(2,1)S(1)} %collective-permute-done.2.refs_1_), channel_id=1, source_target_pairs={{0,24},{4,28},{8,0},{12,4},{16,8},{20,12},{24,16},{28,20},{1,25},{... | collective-permute-start | bytes 786440 | tf_op jit(solution)/shard_map/ppermute | solution.py:218
  25.9 12.9 %collective-permute-start.14 = (bf16[128,1024]{1,0:T(8,128)(2,1)S(1)}, bf16[128,1024]{1,0:T(8,128)(2,1)S(1)}, u32[]{:S(2)}, u32[]{:S(2)}) collective-permute-start(bf16[128,1024]{1,0:T(8,128)(2,1)S(1)} %collective-permute-done.2.refs_1_), channel_id=1, source_target_pairs={{0,8},{4,12},{8,16},{12,20},{16,24},{20,28},{24,0},{28,4},{1,9},{5... | collective-permute-start | bytes 786440 | tf_op jit(solution)/shard_map/ppermute | solution.py:217
  42.1 12.7 %collective-permute-start.6 = (bf16[128,2048]{1,0:T(8,128)(2,1)S(1)}, bf16[128,2048]{1,0:T(8,128)(2,1)S(1)}, u32[]{:S(2)}, u32[]{:S(2)}) collective-permute-start(bf16[128,2048]{1,0:T(8,128)(2,1)S(1)} %pad_maximum_fusion.2.refs_0_), channel_id=1, source_target_pairs={{0,4},{4,0},{8,12},{12,8},{16,20},{20,16},{24,28},{28,24},{1,5},{5... | collective-permute-start | bytes 1572872 | tf_op jit(solution)/shard_map/ppermute | solution.py:216
  42.4 6.9 %collective-permute-start.12 = (bf16[128,1024]{1,0:T(8,128)(2,1)S(1)}, bf16[128,1024]{1,0:T(8,128)(2,1)S(1)}, u32[]{:S(2)}, u32[]{:S(2)}) collective-permute-start(bf16[128,1024]{1,0:T(8,128)(2,1)S(1)} %collective-permute-done.refs_6_), channel_id=1, source_target_pairs={{0,8},{4,12},{8,16},{12,20},{16,24},{20,28},{24,0},{28,4},{1,9},{5... | collective-permute-start | bytes 786440 | tf_op jit(solution)/shard_map/ppermute | solution.py:217
  44.5 5.7 %collective-permute-start.15 = (bf16[128,1024]{1,0:T(8,128)(2,1)S(1)}, bf16[128,1024]{1,0:T(8,128)(2,1)S(1)}, u32[]{:S(2)}, u32[]{:S(2)}) collective-permute-start(bf16[128,1024]{1,0:T(8,128)(2,1)S(1)} %collective-permute-done.11.refs_3_), channel_id=1, source_target_pairs={{0,24},{4,28},{8,0},{12,4},{16,8},{20,12},{24,16},{28,20},{1,25},{... | collective-permute-start | bytes 786440 | tf_op jit(solution)/shard_map/ppermute | solution.py:218
  62.5 5.3 %collective-permute-start.16 = (bf16[512,1024]{1,0:T(8,128)(2,1)S(1)}, bf16[512,1024]{1,0:T(8,128)(2,1)S(1)}, u32[]{:S(2)}, u32[]{:S(2)}) collective-permute-start(bf16[512,1024]{1,0:T(8,128)(2,1)S(1)} %get-tuple-element.99), channel_id=1, source_target_pairs={{0,32},{32,0},{64,96},{96,64},{1,33},{33,1},{65,97},{97,65},{2,34}... | collective-permute-start | bytes 3145736 | tf_op jit(solution)/shard_map/ppermute | solution.py:285
  65.4 25.2 %collective-permute-start.8 = (bf16[128,2048]{1,0:T(8,128)(2,1)S(1)}, bf16[128,2048]{1,0:T(8,128)(2,1)S(1)}, u32[]{:S(2)}, u32[]{:S(2)}) collective-permute-start(bf16[128,2048]{1,0:T(8,128)(2,1)S(1)} %copy-done.8), channel_id=1, source_target_pairs={{0,24},{4,28},{8,0},{12,4},{16,8},{20,12},{24,16},{28,20},{1,25},{... | collective-permute-start | bytes 1572872 | tf_op jit(solution)/shard_map/ppermute | solution.py:218
  67.9 26.2 %collective-permute-start.7 = (bf16[128,2048]{1,0:T(8,128)(2,1)S(1)}, bf16[128,2048]{1,0:T(8,128)(2,1)S(1)}, u32[]{:S(2)}, u32[]{:S(2)}) collective-permute-start(bf16[128,2048]{1,0:T(8,128)(2,1)S(1)} %copy-done.8), channel_id=1, source_target_pairs={{0,8},{4,12},{8,16},{12,20},{16,24},{20,28},{24,0},{28,4},{1,9},{5... | collective-permute-start | bytes 1572872 | tf_op jit(solution)/shard_map/ppermute | solution.py:217
  68.1 26.8 %collective-permute-start.23 = (bf16[256,1024]{1,0:T(8,128)(2,1)S(1)}, bf16[256,1024]{1,0:T(8,128)(2,1)}, u32[]{:S(2)}, u32[]{:S(2)}) collective-permute-start(bf16[256,1024]{1,0:T(8,128)(2,1)S(1)} %add_convert_fusion.3), channel_id=1, source_target_pairs={{0,64},{32,96},{64,0},{96,32},{1,65},{33,97},{65,1},{97,33},{2,66}... | collective-permute-start | bytes 1572872 | tf_op jit(solution)/shard_map/ppermute | solution.py:287
  107.7 27.0 %copy-start.4 = (f32[1024,1024]{1,0:T(8,128)S(1)}, f32[1024,1024]{1,0:T(8,128)}, u32[]{:S(2)}) copy-start(f32[1024,1024]{1,0:T(8,128)} %copy-done.3) | copy-start | bytes 12582916
  113.4 7.6 %collective-permute-start.24 = (bf16[512,2048]{1,0:T(8,128)(2,1)S(1)}, bf16[512,2048]{1,0:T(8,128)(2,1)S(1)}, u32[]{:S(2)}, u32[]{:S(2)}) collective-permute-start(bf16[512,2048]{1,0:T(8,128)(2,1)S(1)} %get-tuple-element.113), channel_id=1, source_target_pairs={{0,32},{32,0},{64,96},{96,64},{1,33},{33,1},{65,97},{97,65},{2,34}... | collective-permute-start | bytes 6291464 | tf_op jit(solution)/shard_map/ppermute | solution.py:285
  114.2 20.5 %copy-start.2 = (bf16[1024,2048]{1,0:T(8,128)(2,1)S(1)}, bf16[1024,2048]{1,0:T(8,128)(2,1)}, u32[]{:S(2)}) copy-start(bf16[1024,2048]{1,0:T(8,128)(2,1)} %all-gather.5.cloned.1.call-done.refs_0_) | copy-start | bytes 12582916
  115.4 14.7 %collective-permute-start.4 = (bf16[128,2048]{1,0:T(8,128)(2,1)S(1)}, bf16[128,2048]{1,0:T(8,128)(2,1)S(1)}, u32[]{:S(2)}, u32[]{:S(2)}) collective-permute-start(bf16[128,2048]{1,0:T(8,128)(2,1)S(1)} %pad_maximum_fusion.refs_0_), channel_id=1, source_target_pairs={{0,4},{4,0},{8,12},{12,8},{16,20},{20,16},{24,28},{28,24},{1,5},{5... | collective-permute-start | bytes 1572872 | tf_op jit(solution)/shard_map/ppermute | solution.py:216
  118.4 14.0 %collective-permute-start.10 = (bf16[128,2048]{1,0:T(8,128)(2,1)S(1)}, bf16[128,2048]{1,0:T(8,128)(2,1)S(1)}, u32[]{:S(2)}, u32[]{:S(2)}) collective-permute-start(bf16[128,2048]{1,0:T(8,128)(2,1)S(1)} %pad_maximum_fusion.refs_0_), channel_id=1, source_target_pairs={{0,8},{4,12},{8,16},{12,20},{16,24},{20,28},{24,0},{28,4},{1,9},{5... | collective-permute-start | bytes 1572872 | tf_op jit(solution)/shard_map/ppermute | solution.py:217
  118.9 13.4 %collective-permute-start.17 = (bf16[128,2048]{1,0:T(8,128)(2,1)S(1)}, bf16[128,2048]{1,0:T(8,128)(2,1)S(1)}, u32[]{:S(2)}, u32[]{:S(2)}) collective-permute-start(bf16[128,2048]{1,0:T(8,128)(2,1)S(1)} %copy-done.11), channel_id=1, source_target_pairs={{0,24},{4,28},{8,0},{12,4},{16,8},{20,12},{24,16},{28,20},{1,25},{... | collective-permute-start | bytes 1572872 | tf_op jit(solution)/shard_map/ppermute | solution.py:218
  122.7 32.9 %copy-start.6 = (bf16[128,2048]{1,0:T(8,128)(2,1)S(1)}, bf16[128,2048]{1,0:T(8,128)(2,1)}, u32[]{:S(2)}) copy-start(bf16[128,2048]{1,0:T(8,128)(2,1)} %copy-done.5) | copy-start | bytes 1572868
  122.7 32.9 %copy-start.9 = (bf16[128,2048]{1,0:T(8,128)(2,1)S(1)}, bf16[128,2048]{1,0:T(8,128)(2,1)}, u32[]{:S(2)}) copy-start(bf16[128,2048]{1,0:T(8,128)(2,1)} %copy-done.7) | copy-start | bytes 1572868
  122.7 32.9 %copy-start.14 = (bf16[128,2048]{1,0:T(8,128)(2,1)S(1)}, bf16[128,2048]{1,0:T(8,128)(2,1)}, u32[]{:S(2)}) copy-start(bf16[128,2048]{1,0:T(8,128)(2,1)} %copy-done.13) | copy-start | bytes 1572868
  122.7 32.9 %collective-permute-start.25 = (bf16[256,2048]{1,0:T(8,128)(2,1)}, bf16[256,2048]{1,0:T(8,128)(2,1)}, u32[]{:S(2)}, u32[]{:S(2)}) collective-permute-start(bf16[256,2048]{1,0:T(8,128)(2,1)} %add_convert_fusion.2), channel_id=1, source_target_pairs={{0,64},{32,96},{64,0},{96,32},{1,65},{33,97},{65,1},{97,33},{2,66}... | collective-permute-start | bytes 3145736 | tf_op jit(solution)/shard_map/ppermute | solution.py:287
  123.2 20.4 %collective-permute-start.22 = (bf16[128,2048]{1,0:T(8,128)(2,1)S(1)}, bf16[128,2048]{1,0:T(8,128)(2,1)S(1)}, u32[]{:S(2)}, u32[]{:S(2)}) collective-permute-start(bf16[128,2048]{1,0:T(8,128)(2,1)S(1)} %collective-permute-done.5.refs_6_), channel_id=1, source_target_pairs={{0,8},{4,12},{8,16},{12,20},{16,24},{20,28},{24,0},{28,4},{1,9},{5... | collective-permute-start | bytes 1572872 | tf_op jit(solution)/shard_map/ppermute | solution.py:217
  130.1 13.5 %collective-permute-start.9 = (bf16[128,2048]{1,0:T(8,128)(2,1)S(1)}, bf16[128,2048]{1,0:T(8,128)(2,1)S(1)}, u32[]{:S(2)}, u32[]{:S(2)}) collective-permute-start(bf16[128,2048]{1,0:T(8,128)(2,1)S(1)} %pad_maximum_fusion.refs_0_), channel_id=1, source_target_pairs={{0,24},{4,28},{8,0},{12,4},{16,8},{20,12},{24,16},{28,20},{1,25},{... | collective-permute-start | bytes 1572872 | tf_op jit(solution)/shard_map/ppermute | solution.py:218
  132.3 50.6 %copy-start.15 = (bf16[128,2048]{1,0:T(8,128)(2,1)}, bf16[128,2048]{1,0:T(8,128)(2,1)S(1)}, u32[]{:S(2)}) copy-start(bf16[128,2048]{1,0:T(8,128)(2,1)S(1)} %collective-permute-done.10.refs_6_) | copy-start | bytes 1572868
  132.3 23.3 %copy-start.19 = (bf16[128,2048]{1,0:T(8,128)(2,1)}, bf16[128,2048]{1,0:T(8,128)(2,1)S(1)}, u32[]{:S(2)}) copy-start(bf16[128,2048]{1,0:T(8,128)(2,1)S(1)} %collective-permute-done.17.refs_5_) | copy-start | bytes 1572868
  132.3 21.7 %collective-permute-start.18 = (bf16[128,2048]{1,0:T(8,128)(2,1)S(1)}, bf16[128,2048]{1,0:T(8,128)(2,1)S(1)}, u32[]{:S(2)}, u32[]{:S(2)}) collective-permute-start(bf16[128,2048]{1,0:T(8,128)(2,1)S(1)} %collective-permute-done.4.refs_1_), channel_id=1, source_target_pairs={{0,24},{4,28},{8,0},{12,4},{16,8},{20,12},{24,16},{28,20},{1,25},{... | collective-permute-start | bytes 1572872 | tf_op jit(solution)/shard_map/ppermute | solution.py:218
  134.7 20.1 %collective-permute-start.21 = (bf16[128,2048]{1,0:T(8,128)(2,1)S(1)}, bf16[128,2048]{1,0:T(8,128)(2,1)S(1)}, u32[]{:S(2)}, u32[]{:S(2)}) collective-permute-start(bf16[128,2048]{1,0:T(8,128)(2,1)S(1)} %collective-permute-done.4.refs_1_), channel_id=1, source_target_pairs={{0,8},{4,12},{8,16},{12,20},{16,24},{20,28},{24,0},{28,4},{1,9},{5... | collective-permute-start | bytes 1572872 | tf_op jit(solution)/shard_map/ppermute | solution.py:217
  143.6 39.4 %copy-start.17 = (bf16[128,2048]{1,0:T(8,128)(2,1)}, bf16[128,2048]{1,0:T(8,128)(2,1)S(1)}, u32[]{:S(2)}) copy-start(bf16[128,2048]{1,0:T(8,128)(2,1)S(1)} %collective-permute-done.9.refs_2_) | copy-start | bytes 1572868
  154.0 28.9 %copy-start.21 = (bf16[128,2048]{1,0:T(8,128)(2,1)}, bf16[128,2048]{1,0:T(8,128)(2,1)S(1)}, u32[]{:S(2)}) copy-start(bf16[128,2048]{1,0:T(8,128)(2,1)S(1)} %collective-permute-done.18.refs_3_) | copy-start | bytes 1572868
  162.4 5.4 %collective-permute-start.26 = (bf16[512,2048]{1,0:T(8,128)(2,1)S(1)}, bf16[512,2048]{1,0:T(8,128)(2,1)S(1)}, u32[]{:S(2)}, u32[]{:S(2)}) collective-permute-start(bf16[512,2048]{1,0:T(8,128)(2,1)S(1)} %get-tuple-element.124), channel_id=1, source_target_pairs={{0,32},{32,0},{64,96},{96,64},{1,33},{33,1},{65,97},{97,65},{2,34}... | collective-permute-start | bytes 6291464 | tf_op jit(solution)/shard_map/ppermute | solution.py:285
  168.2 25.5 %collective-permute-start.30 = (bf16[256,2048]{1,0:T(8,128)(2,1)S(1)}, bf16[256,2048]{1,0:T(8,128)(2,1)S(1)}, u32[]{:S(2)}, u32[]{:S(2)}) collective-permute-start(bf16[256,2048]{1,0:T(8,128)(2,1)S(1)} %add_convert_fusion.1), channel_id=1, source_target_pairs={{0,64},{32,96},{64,0},{96,32},{1,65},{33,97},{65,1},{97,33},{2,66}... | collective-permute-start | bytes 3145736 | tf_op jit(solution)/shard_map/ppermute | solution.py:287
  168.9 14.0 %collective-permute-start.19 = (bf16[128,2048]{1,0:T(8,128)(2,1)S(1)}, bf16[128,2048]{1,0:T(8,128)(2,1)S(1)}, u32[]{:S(2)}, u32[]{:S(2)}) collective-permute-start(bf16[128,2048]{1,0:T(8,128)(2,1)S(1)} %collective-permute-done.10.refs_6_), channel_id=1, source_target_pairs={{0,8},{4,12},{8,16},{12,20},{16,24},{20,28},{24,0},{28,4},{1,9},{5... | collective-permute-start | bytes 1572872 | tf_op jit(solution)/shard_map/ppermute | solution.py:217
  169.5 13.5 %collective-permute-start.20 = (bf16[128,2048]{1,0:T(8,128)(2,1)S(1)}, bf16[128,2048]{1,0:T(8,128)(2,1)S(1)}, u32[]{:S(2)}, u32[]{:S(2)}) collective-permute-start(bf16[128,2048]{1,0:T(8,128)(2,1)S(1)} %collective-permute-done.18.refs_3_), channel_id=1, source_target_pairs={{0,24},{4,28},{8,0},{12,4},{16,8},{20,12},{24,16},{28,20},{1,25},{... | collective-permute-start | bytes 1572872 | tf_op jit(solution)/shard_map/ppermute | solution.py:218
  206.5 8.3 %collective-permute-start.31 = (bf16[512,2048]{1,0:T(8,128)(2,1)}, bf16[512,2048]{1,0:T(8,128)(2,1)S(1)}, u32[]{:S(2)}, u32[]{:S(2)}) collective-permute-start(bf16[512,2048]{1,0:T(8,128)(2,1)} %get-tuple-element.154), channel_id=1, source_target_pairs={{0,32},{32,0},{64,96},{96,64},{1,33},{33,1},{65,97},{97,65},{2,34}... | collective-permute-start | bytes 6291464 | tf_op jit(solution)/shard_map/ppermute | solution.py:285
  210.6 14.8 %collective-permute-start.27 = (bf16[256,1024]{1,0:T(8,128)(2,1)S(1)}, bf16[256,1024]{1,0:T(8,128)(2,1)S(1)}, u32[]{:S(2)}, u32[]{:S(2)}) collective-permute-start(bf16[256,1024]{1,0:T(8,128)(2,1)S(1)} %copy-done.57), channel_id=1, source_target_pairs={{0,1},{1,2},{2,3},{3,0},{4,5},{5,6},{6,7},{7,4},{8,9},{9,10},{10,1... | collective-permute-start | bytes 1572872 | tf_op jit(solution)/shard_map/ppermute | solution.py:278
  211.8 13.6 %collective-permute-start.28 = (bf16[256,1024]{1,0:T(8,128)(2,1)S(1)}, bf16[256,1024]{1,0:T(8,128)(2,1)S(1)}, u32[]{:S(2)}, u32[]{:S(2)}) collective-permute-start(bf16[256,1024]{1,0:T(8,128)(2,1)S(1)} %copy-done.55), channel_id=1, source_target_pairs={{0,3},{1,0},{2,1},{3,2},{4,7},{5,4},{6,5},{7,6},{8,11},{9,8},{10,9... | collective-permute-start | bytes 1572872 | tf_op jit(solution)/shard_map/ppermute | solution.py:279
  213.3 24.2 %collective-permute-start.29 = (bf16[256,1024]{1,0:T(8,128)(2,1)S(1)}, bf16[256,1024]{1,0:T(8,128)(2,1)S(1)}, u32[]{:S(2)}, u32[]{:S(2)}) collective-permute-start(bf16[256,1024]{1,0:T(8,128)(2,1)S(1)} %copy-done.53), channel_id=1, source_target_pairs={{0,2},{1,3},{2,0},{3,1},{4,6},{5,7},{6,4},{7,5},{8,10},{9,11},{10,... | collective-permute-start | bytes 1572872 | tf_op jit(solution)/shard_map/ppermute | solution.py:280
  215.2 22.3 %copy-start.51 = (bf16[256,1024]{1,0:T(8,128)(2,1)S(1)}, bf16[256,1024]{1,0:T(8,128)(2,1)}, u32[]{:S(2)}) copy-start(bf16[256,1024]{1,0:T(8,128)(2,1)} %copy-done.50) | copy-start | bytes 1572868
  215.2 24.3 %collective-permute-start.32 = (bf16[256,2048]{1,0:T(8,128)(2,1)S(1)}, bf16[256,2048]{1,0:T(8,128)(2,1)S(1)}, u32[]{:S(2)}, u32[]{:S(2)}) collective-permute-start(bf16[256,2048]{1,0:T(8,128)(2,1)S(1)} %add_convert_fusion), channel_id=1, source_target_pairs={{0,64},{32,96},{64,0},{96,32},{1,65},{33,97},{65,1},{97,33},{2,66}... | collective-permute-start | bytes 3145736 | tf_op jit(solution)/shard_map/ppermute | solution.py:287
  216.5 22.4 %copy-start.61 = (bf16[512,2048]{1,0:T(8,128)(2,1)S(1)}, bf16[512,2048]{1,0:T(8,128)(2,1)}, u32[]{:S(2)}) copy-start(bf16[512,2048]{1,0:T(8,128)(2,1)} %copy-done.60) | copy-start | bytes 6291460
  218.5 20.4 %copy-start.31 = (bf16[512,2048]{1,0:T(8,128)(2,1)S(1)}, bf16[512,2048]{1,0:T(8,128)(2,1)}, u32[]{:S(2)}) copy-start(bf16[512,2048]{1,0:T(8,128)(2,1)} %copy-done.30) | copy-start | bytes 6291460
  (55 other events, 215.0 us)
Sparse Core Ops, SparseCore 0:
  9.7 33.9 all-gather.2
  45.9 59.5 all-gather.4

commit v2 on v1

--- a/solution.py
+++ b/solution.py
@@ -10,9 +10,6 @@
 ROW_UP = [(i, (i + 2) % 8) for i in range(8)]
 ROW_DOWN = [(i, (i - 2) % 8) for i in range(8)]
 ROW_SWAP = [(i, i ^ 1) for i in range(8)]
-COL_UP = [(i, (i + 1) % 4) for i in range(4)]
-COL_DOWN = [(i, (i - 1) % 4) for i in range(4)]
-COL_FAR = [(i, (i + 2) % 4) for i in range(4)]
 CORE_SWAP = [(i, i ^ 1) for i in range(4)]
 PAIR_SWAP = [(i, i ^ 2) for i in range(4)]
 
@@ -116,7 +113,6 @@
     tile = width // TILES
     half = TILES // 2
     column = start // w
-    block = tokens // 4
     with_weight, with_input = input_columns is not None, gate_weight is not None
 
     def kernel(places_ref, *refs):
@@ -127,7 +123,7 @@
         weight_refs = take(2) if with_input else []
         total_refs = take(1) if total is not None else []
         part_refs = take(2) if with_weight else []
-        sum_refs = take(4 if last else 1) if with_input else []
+        sum_refs = take(1) if with_input else []
         if count > 1:
             rows_ref = refs.pop(0)
 
@@ -155,14 +151,7 @@
             term += lax.dot_general(rows_ref[:, w:], weight_refs[1][...], across, preferred_element_type=jnp.float32)
             if total_refs:
                 term += total_refs[0][...]
-            if last:
-                sum_ref = refs.pop(0)
-                sum_ref[...] = term
-                for k in range(4):
-                    at = pl.multiple_of(places_ref[8 + k] * block, block)
-                    sum_refs[k][...] = sum_ref[pl.ds(at, block), :].astype(jnp.bfloat16)
-            else:
-                sum_refs[0][...] = term
+            sum_refs[0][...] = term.astype(sum_refs[0].dtype)
 
     in_specs = [pl.BlockSpec((rows, hidden), lambda i, _: (0, 0), pipeline_mode=pl.Buffered(1))] * count
     operands = [*pieces]
@@ -183,13 +172,8 @@
         if total is not None:
             in_specs.append(pl.BlockSpec((tokens, tile), lambda i, _: (0, i)))
             operands.append(total)
-        if last:
-            out_shape += [jax.ShapeDtypeStruct((block, width), jnp.bfloat16)] * 4
-            out_specs += [pl.BlockSpec((block, tile), lambda i, _: (0, i))] * 4
-            scratch.append(pltpu.VMEM((tokens, tile), jnp.float32))
-        else:
-            out_shape.append(jax.ShapeDtypeStruct((tokens, width), jnp.float32))
-            out_specs.append(pl.BlockSpec((tokens, tile), lambda i, _: (0, i)))
+        out_shape.append(jax.ShapeDtypeStruct((tokens, width), jnp.bfloat16 if last else jnp.float32))
+        out_specs.append(pl.BlockSpec((tokens, tile), lambda i, _: (0, i)))
     return pl.pallas_call(
         kernel,
         out_shape=tuple(out_shape),
@@ -203,15 +187,14 @@
 
 
 def body(layer_input, hidden_grad, gate_pre, up_pre, gate_weight, up_weight):
-    row, col, dp = lax.axis_index("row"), lax.axis_index("col"), lax.axis_index("dp")
+    row, dp = lax.axis_index("row"), lax.axis_index("dp")
     y, z_hi = row // 2, row % 2
     tokens, width = layer_input.shape
     quarter = width // 4
     count = len(CHUNKS)
     steps = jnp.arange(4, dtype=jnp.int32)
     blocks = (y + steps) % 4
-    places = jnp.concatenate([jnp.stack([2 * blocks, 2 * blocks + 1], axis=1).reshape(8), (col + steps) % 4])
-    places = places.astype(jnp.int32)
+    places = jnp.stack([2 * blocks, 2 * blocks + 1], axis=1).reshape(8).astype(jnp.int32)
 
     swap = lambda value: lax.ppermute(value, "row", ROW_SWAP)
     up = lambda value: lax.ppermute(value, "row", ROW_UP)
@@ -243,7 +226,7 @@
     far[2] = up(after(below[2], *second))
     whole_1 = join_rows(steps[:2], after_all([own[1], other[1]], *second))
     rows[1] = gather(whole_1)
-    third = (far[0], other_far[0], other[2])
+    third = (far[0], other_far[0], other[2], other[3])
     input_columns = order_input(after(group_input, *third, whole_1), row, dp)
     other_below[2], other_above[2] = up(other[2]), down(other[2])
     own_3 = after(own[3], other_below[2], other_above[2])
@@ -254,7 +237,7 @@
     gate_out = jnp.zeros((quarter, gate_weight.shape[1]), jnp.bfloat16)
     up_out = jnp.zeros((quarter, gate_weight.shape[1]), jnp.bfloat16)
     total = None
-    chip_send, pair_parts = [None] * count, [None] * count
+    chip_send, pair_parts, finishes = [None] * count, [None] * count, [None] * count
     for c, (s, w, gathered) in enumerate(CHUNKS):
         earlier = [*before[c]]
         if c >= 1:
@@ -269,17 +252,11 @@
             own[c], other[c], above[c], other_above[c], far[c], other_far[c], below[c], other_below[c]
         ]
         if c == count - 1:
-            shares = chunk_grads(
+            (input_part,) = chunk_grads(
                 places, after_all(pieces, chip_send[c - 1], total), None, gate_weight, up_weight, s, total, True
             )
-            mine, next_one, across, last_one = shares
-            shares = (
-                mine,
-                lax.ppermute(next_one, "col", COL_UP),
-                lax.ppermute(last_one, "col", COL_DOWN),
-                lax.ppermute(across, "col", COL_FAR),
-            )
-            earlier += shares[:1]
+            gate_out, up_out = after_all([gate_out, up_out], total)
+            earlier += [input_part, gate_out, up_out]
         pieces = after_all(pieces, *earlier)
         send, keep = chunk_grads(places, pieces, input_columns, None, None, s, None, False)
         core_part = lax.ppermute(send, "dp", CORE_SWAP)
@@ -289,16 +266,19 @@
             pieces = after_all(pieces, chip_send[c])
             (total,) = chunk_grads(places, pieces, None, gate_weight, up_weight, s, total, False)
 
-        def finish(columns):
+        def finish(columns, keep=keep, core_part=core_part, pair_part=pair_part):
             value = keep[quarter:, columns].astype(jnp.float32) + core_part[quarter:, columns].astype(jnp.float32)
             return ((value + pair_part[:, columns].astype(jnp.float32)) * inverse_groups).astype(jnp.bfloat16)
 
-        gate_out = lax.dynamic_update_slice(gate_out, finish(slice(0, w)), (0, s))
-        up_out = lax.dynamic_update_slice(up_out, finish(slice(w, 2 * w)), (0, s))
-
-    input_grad = sum(share.astype(jnp.float32) for share in shares)
+        finishes[c] = finish
+        for k in ([c - 1] if c else []) + ([c] if c == count - 1 else []):
+            start, hidden = CHUNKS[k][:2]
+            gate_out = lax.dynamic_update_slice(gate_out, finishes[k](slice(0, hidden)), (0, start))
+            up_out = lax.dynamic_update_slice(up_out, finishes[k](slice(hidden, 2 * hidden)), (0, start))
+
+    input_grad = lax.psum_scatter(input_part, "col", scatter_dimension=0, tiled=True)
     halves = input_grad.reshape(2, tokens // 2, width)
-    input_grad = jnp.where(z_hi == 0, halves, halves[::-1]).reshape(tokens, width).astype(jnp.bfloat16)
+    input_grad = jnp.where(z_hi == 0, halves, halves[::-1]).reshape(tokens, width)
     return input_grad, gate_out, up_out
 
 

time: 250 us -> 238 us (0.952)
  waiting for transfers between devices: 92.7 us -> 84.1 us
  other arithmetic: 14.7 us -> 18.6 us
  local copies, waits for them, and re-layouts: 30.1 us -> 26.7 us
    ppermute x3 -> x0, waiting for transfers between devices: 19 us -> none  [the longest x1 12.1 us: body(): lax.ppermute(across, 'col', COL_FAR)]
    ppermute x4, waiting for transfers between devices: 0.01 us -> 10.7 us  [body(): pair_part = pair_parts[c] = lax.ppermute(chip_send[c], 'dp', PAIR_SWAP)]
    all_gather x1, waiting for transfers between devices: 10.6 us -> 0.43 us  [body(): lax.all_gather(value, 'row', axis=0, tiled=True, axis_index_groups=SAME_Z)]
    reduce_scatter x0 -> x1, waiting for transfers between devices: none -> 7.54 us  [body(): lax.psum_scatter(input_part, 'col', scatter_dimension=0, tiled=True)]
    ppermute x3 -> x0, starting transfers between devices: 4.16 us -> none  [the longest x1 1.49 us: body(): lax.ppermute(last_one, 'col', COL_DOWN)]
    dynamic_update_slice x3, other arithmetic: 3.31 us -> 7.27 us  [body(): lax.dynamic_update_slice(up_out, finishes[k](slice(hidden, 2 * hidden)),...]
    unnamed x136 -> x132, local copies, waits for them, and re-layouts: 29.8 us -> 26.4 us
    ppermute x9, starting transfers between devices: 17.1 us -> 19.6 us  [body(): down = lambda value: lax.ppermute(value, 'row', ROW_DOWN)]
  transfers between devices with their start and end apart: 35 -> 33, of which waited for: 17 -> 18; matrix products, arithmetic and copies ran while one was open for 6% -> 7% of each run, Pallas kernels for 13% -> 16%
where the time goes in v2:
time: 238 us; the launch traced here: 237 us
  waiting for transfers between devices  84.1 us (35%)
  Pallas kernels  50.2 us (21%)
  starting transfers between devices  43.4 us (18%)
  local copies, waits for them, and re-layouts  26.7 us (11%)
  other arithmetic  18.6 us (8%)
  between operations  14.4 us (6%)
    pallas_call x8, Pallas kernels, chunk_grads(): pl.pallas_call(kernel, out_shape=tuple(out_shape), grid_spec=pltpu.Prefet...  47.4 us
    ppermute x9, waiting for transfers between devices, body(): down = lambda value: lax.ppermute(value, 'row', ROW_DOWN)  31 us
    unnamed x132, local copies, waits for them, and re-layouts  26.4 us
    ppermute x9, starting transfers between devices, body(): down = lambda value: lax.ppermute(value, 'row', ROW_DOWN)  19.6 us
    ppermute x9, waiting for transfers between devices, body(): up = lambda value: lax.ppermute(value, 'row', ROW_UP)  15.1 us
    ppermute x4, waiting for transfers between devices, body(): swap = lambda value: lax.ppermute(value, 'row', ROW_SWAP)  12.7 us
    ppermute x4, waiting for transfers between devices, body(): pair_part = pair_parts[c] = lax.ppermute(chip_send[c], 'dp', PAIR_SWAP)  10.7 us
    ppermute x4, starting transfers between devices, body(): swap = lambda value: lax.ppermute(value, 'row', ROW_SWAP)  9.09 us
  transfers between devices with their start and end apart: 33, of which 18 were waited for; matrix products, arithmetic and copies ran while one was open for 7% of the time, Pallas kernels for 16%

profile of v2, /device:TPU:1, one launch (start us, length us, event | category | flops | bytes accessed | tf_op | source)
XLA Modules:
  0.0 237.4 jit_solution(7471675072302925740)
XLA Ops:
  9.2 2.2 collective-permute-start
  11.4 1.5 collective-permute-start.1
  12.9 3.6 %collective-permute-start.2 = (bf16[128,1024]{1,0:T(8,128)(2,1)S(1)}, bf16[128,1024]{1,0:T(8,128)(2,1)S(1)}, u32[]{:S(2)}, u32[]{:S(2)}) collective-permute-start(bf16[128,1024]{1,0:T(8,128)(2,1)S(1)} %pad_maximum_fusion.3.refs_0_), channel_id=1, source_target_pairs={{0,4},{4,0},{8,12},{12,8},{16,20},{20,16},{24,28},{28,24},{1,5},{5... | collective-permute-start | bytes 786440 | tf_op jit(solution)/shard_map/ppermute | solution.py:199
  16.5 2.2 fusion.8
  18.8 2.7 %collective-permute-start.13 = (bf16[128,2048]{1,0:T(8,128)(2,1)S(1)}, bf16[128,2048]{1,0:T(8,128)(2,1)S(1)}, u32[]{:S(2)}, u32[]{:S(2)}) collective-permute-start(bf16[128,2048]{1,0:T(8,128)(2,1)S(1)} %pad_maximum_fusion.2.refs_0_), channel_id=1, source_target_pairs={{0,24},{4,28},{8,0},{12,4},{16,8},{20,12},{24,16},{28,20},{1,25},{... | collective-permute-start | bytes 1572872 | tf_op jit(solution)/shard_map/ppermute | solution.py:201
  22.2 2.4 %collective-permute-start.3 = (bf16[128,2048]{1,0:T(8,128)(2,1)S(1)}, bf16[128,2048]{1,0:T(8,128)(2,1)S(1)}, u32[]{:S(2)}, u32[]{:S(2)}) collective-permute-start(bf16[128,2048]{1,0:T(8,128)(2,1)S(1)} %pad_maximum_fusion.1.refs_0_), channel_id=1, source_target_pairs={{0,4},{4,0},{8,12},{12,8},{16,20},{20,16},{24,28},{28,24},{1,5},{5... | collective-permute-start | bytes 1572872 | tf_op jit(solution)/shard_map/ppermute | solution.py:199
  26.9 9.8 %collective-permute-done.11.refs_3_ = bf16[128,1024]{1,0:T(8,128)(2,1)S(1)} collective-permute-done((bf16[128,1024]{1,0:T(8,128)(2,1)S(1)}, bf16[128,1024]{1,0:T(8,128)(2,1)S(1)}, u32[]{:S(2)}, u32[]{:S(2)}) %collective-permute-start.11) | collective-permute-done | bytes 262176 | tf_op jit(solution)/shard_map/ppermute | solution.py:201
  39.3 1.6 join_rows.1
  41.1 1.5 collective-permute-start.6
  42.6 1.6 collective-permute-start.4
  45.0 2.7 %collective-permute-start.15 = (bf16[128,1024]{1,0:T(8,128)(2,1)S(1)}, bf16[128,1024]{1,0:T(8,128)(2,1)S(1)}, u32[]{:S(2)}, u32[]{:S(2)}) collective-permute-start(bf16[128,1024]{1,0:T(8,128)(2,1)S(1)} %collective-permute-done.11.refs_3_), channel_id=1, source_target_pairs={{0,24},{4,28},{8,0},{12,4},{16,8},{20,12},{24,16},{28,20},{1,25},{... | collective-permute-start | bytes 786440 | tf_op jit(solution)/shard_map/ppermute | solution.py:201
  48.4 2.5 %collective-permute-done.12.refs_4_ = bf16[128,1024]{1,0:T(8,128)(2,1)S(1)} collective-permute-done((bf16[128,1024]{1,0:T(8,128)(2,1)S(1)}, bf16[128,1024]{1,0:T(8,128)(2,1)S(1)}, u32[]{:S(2)}, u32[]{:S(2)}) %collective-permute-start.12) | collective-permute-done | bytes 262176 | tf_op jit(solution)/shard_map/ppermute | solution.py:200
  52.4 1.5 collective-permute-done.6.refs_1_
  53.9 11.2 %collective-permute-done.4.refs_1_ = bf16[128,2048]{1,0:T(8,128)(2,1)S(1)} collective-permute-done((bf16[128,2048]{1,0:T(8,128)(2,1)S(1)}, bf16[128,2048]{1,0:T(8,128)(2,1)S(1)}, u32[]{:S(2)}, u32[]{:S(2)}) %collective-permute-start.4) | collective-permute-done | bytes 524320 | tf_op jit(solution)/shard_map/ppermute | solution.py:199
  65.9 1.6 copy-done.34
  69.0 3.4 %chunk_grads.8 = (bf16[512,1024]{1,0:T(8,128)(2,1)S(1)}, bf16[512,1024]{1,0:T(8,128)(2,1)S(1)}) custom-call(s32[8]{0:T(128)S(1)} %reshape.62.places_ref, bf16[128,1024]{1,0:T(8,128)(2,1)S(1)} %pad_maximum_fusion.3.refs_0_, bf16[128,1024]{1,0:T(8,128)(2,1)S(1)} %copy-done.45, bf16[128,1024]{1,0:T(8,128)(2,1)S(1)} %copy-done.43, ...), custom_call_target="tpu_custom_call" | custom-call | tf_op jit(solution)/shard_map/chunk_grads/pallas_call | solution.py:177
  72.4 3.2 %collective-permute-start.16 = (bf16[512,1024]{1,0:T(8,128)(2,1)S(1)}, bf16[512,1024]{1,0:T(8,128)(2,1)S(1)}, u32[]{:S(2)}, u32[]{:S(2)}) collective-permute-start(bf16[512,1024]{1,0:T(8,128)(2,1)S(1)} %get-tuple-element.97), channel_id=1, source_target_pairs={{0,32},{32,0},{64,96},{96,64},{1,33},{33,1},{65,97},{97,65},{2,34}... | collective-permute-start | bytes 3145736 | tf_op jit(solution)/shard_map/ppermute | solution.py:262
  75.7 2.4 %collective-permute-start.8 = (bf16[128,2048]{1,0:T(8,128)(2,1)S(1)}, bf16[128,2048]{1,0:T(8,128)(2,1)S(1)}, u32[]{:S(2)}, u32[]{:S(2)}) collective-permute-start(bf16[128,2048]{1,0:T(8,128)(2,1)S(1)} %copy-done.16), channel_id=1, source_target_pairs={{0,24},{4,28},{8,0},{12,4},{16,8},{20,12},{24,16},{28,20},{1,25},{... | collective-permute-start | bytes 1572872 | tf_op jit(solution)/shard_map/ppermute | solution.py:201
  79.8 3.2 %copy-done = bf16[1024,3584]{1,0:T(8,128)(2,1)S(1)} copy-done((bf16[1024,3584]{1,0:T(8,128)(2,1)S(1)}, bf16[1024,3584]{1,0:T(8,128)(2,1)}, u32[]{:S(2)}) %copy-start) | copy-done | bytes 7340056
  83.0 4.6 %chunk_grads.9.refs_3_ = f32[1024,1024]{1,0:T(8,128)S(1)} custom-call(s32[8]{0:T(128)S(1)} %reshape.62.places_ref, bf16[128,1024]{1,0:T(8,128)(2,1)S(1)} %pad_maximum_fusion.3.refs_0_, bf16[128,1024]{1,0:T(8,128)(2,1)S(1)} %copy-done.45, bf16[128,1024]{1,0:T(8,128)(2,1)S(1)} %copy-done.43, bf16[128,1024]{1,0:T(8,128)(2,1)S(1)} %copy-done.47, ...), custom_call_target="tpu_custom_call" | custom-call | tf_op jit(solution)/shard_map/chunk_grads/pallas_call | solution.py:177
  87.6 2.0 copy-done.3
  89.6 11.2 %collective-permute-done.8.refs_3_ = bf16[128,2048]{1,0:T(8,128)(2,1)S(1)} collective-permute-done((bf16[128,2048]{1,0:T(8,128)(2,1)S(1)}, bf16[128,2048]{1,0:T(8,128)(2,1)S(1)}, u32[]{:S(2)}, u32[]{:S(2)}) %collective-permute-start.8) | collective-permute-done | bytes 524320 | tf_op jit(solution)/shard_map/ppermute | solution.py:201
  100.9 3.4 %collective-permute-done.7.refs_7_ = bf16[128,2048]{1,0:T(8,128)(2,1)S(1)} collective-permute-done((bf16[128,2048]{1,0:T(8,128)(2,1)S(1)}, bf16[128,2048]{1,0:T(8,128)(2,1)S(1)}, u32[]{:S(2)}, u32[]{:S(2)}) %collective-permute-start.7) | collective-permute-done | bytes 524320 | tf_op jit(solution)/shard_map/ppermute | solution.py:200
  105.5 2.2 copy-done.1
  107.7 5.6 %chunk_grads.10 = (bf16[512,2048]{1,0:T(8,128)(2,1)S(1)}, bf16[512,2048]{1,0:T(8,128)(2,1)S(1)}) custom-call(s32[8]{0:T(128)S(1)} %reshape.62.places_ref, bf16[1024,2048]{1,0:T(8,128)(2,1)S(1)} %copy-done.1, bf16[1024,1024]{1,0:T(8,128)(2,1)S(1)} %order_input.1.refs_8_.refs_1_), custom_call_target="tpu_custom_call" | custom-call | tf_op jit(solution)/shard_map/chunk_grads/pallas_call | solution.py:177
  114.7 2.1 collective-permute-start.17
  118.4 1.4 collective-permute-start.25
  120.3 2.1 collective-permute-start.9
  122.4 6.4 %collective-permute-done.10.refs_6_ = bf16[128,2048]{1,0:T(8,128)(2,1)S(1)} collective-permute-done((bf16[128,2048]{1,0:T(8,128)(2,1)S(1)}, bf16[128,2048]{1,0:T(8,128)(2,1)S(1)}, u32[]{:S(2)}, u32[]{:S(2)}) %collective-permute-start.10) | collective-permute-done | bytes 524320 | tf_op jit(solution)/shard_map/ppermute | solution.py:200
  128.8 2.6 %collective-permute-start.18 = (bf16[128,2048]{1,0:T(8,128)(2,1)S(1)}, bf16[128,2048]{1,0:T(8,128)(2,1)S(1)}, u32[]{:S(2)}, u32[]{:S(2)}) collective-permute-start(bf16[128,2048]{1,0:T(8,128)(2,1)S(1)} %copy-done.13), channel_id=1, source_target_pairs={{0,24},{4,28},{8,0},{12,4},{16,8},{20,12},{24,16},{28,20},{1,25},{... | collective-permute-start | bytes 1572872 | tf_op jit(solution)/shard_map/ppermute | solution.py:201
  131.4 7.1 %chunk_grads.11.refs_10_ = f32[1024,1024]{1,0:T(8,128)S(1)} custom-call(s32[8]{0:T(128)S(1)} %reshape.62.places_ref, bf16[1024,2048]{1,0:T(8,128)(2,1)S(1)} %copy-done.2, bf16[1024,3584]{1,0:T(8,128)(2,1)} %refs_8_.5, bf16[1024,3584]{1,0:T(8,128)(2,1)} %refs_9_.5, f32[1024,1024]{1,0:T(8,128)S(1)} %copy-done.4), custom_call_target="tpu_custom_call" | custom-call | tf_op jit(solution)/shard_map/chunk_grads/pallas_call | solution.py:177
  138.6 2.0 copy-done.5
  140.6 10.0 %collective-permute-done.18.refs_3_ = bf16[128,2048]{1,0:T(8,128)(2,1)S(1)} collective-permute-done((bf16[128,2048]{1,0:T(8,128)(2,1)S(1)}, bf16[128,2048]{1,0:T(8,128)(2,1)S(1)}, u32[]{:S(2)}, u32[]{:S(2)}) %collective-permute-start.18) | collective-permute-done | bytes 524320 | tf_op jit(solution)/shard_map/ppermute | solution.py:201
  151.4 5.9 %chunk_grads.12 = (bf16[512,2048]{1,0:T(8,128)(2,1)S(1)}, bf16[512,2048]{1,0:T(8,128)(2,1)S(1)}) custom-call(s32[8]{0:T(128)S(1)} %reshape.62.places_ref, bf16[128,2048]{1,0:T(8,128)(2,1)S(1)} %pad_maximum_fusion.2.refs_0_, bf16[128,2048]{1,0:T(8,128)(2,1)S(1)} %copy-done.17, bf16[128,2048]{1,0:T(8,128)(2,1)S(1)} %copy-done.11, ...), custom_call_target="tpu_custom_call" | custom-call | tf_op jit(solution)/shard_map/chunk_grads/pallas_call | solution.py:177
  158.8 2.4 collective-permute-start.20
  162.1 1.7 add_convert_fusion.1
  165.0 7.4 %chunk_grads.13.refs_10_ = f32[1024,1024]{1,0:T(8,128)S(1)} custom-call(s32[8]{0:T(128)S(1)} %reshape.62.places_ref, bf16[128,2048]{1,0:T(8,128)(2,1)S(1)} %pad_maximum_fusion.2.refs_0_, bf16[128,2048]{1,0:T(8,128)(2,1)S(1)} %copy-done.17, bf16[128,2048]{1,0:T(8,128)(2,1)S(1)} %copy-done.11, bf16[128,2048]{1,0:T(8,128)(2,1)S(1)} %copy-done.21, ...), custom_call_target="tpu_custom_call" | custom-call | tf_op jit(solution)/shard_map/chunk_grads/pallas_call | solution.py:177
  173.4 7.3 %chunk_grads.14 = bf16[1024,1024]{1,0:T(8,128)(2,1)S(1)} custom-call(s32[8]{0:T(128)S(1)} %reshape.62.places_ref, bf16[128,2048]{1,0:T(8,128)(2,1)S(1)} %pad_maximum_fusion.refs_0_, bf16[128,2048]{1,0:T(8,128)(2,1)S(1)} %copy-done.13, bf16[128,2048]{1,0:T(8,128)(2,1)S(1)} %collective-permute-done.9.refs_2_, ...), custom_call_target="tpu_custom_call" | custom-call | tf_op jit(solution)/shard_map/chunk_grads/pallas_call | solution.py:177
  183.6 1.7 multiply_convert_fusion.6
  185.6 1.3 copy-done.36
  190.5 5.9 %chunk_grads.15 = (bf16[512,2048]{1,0:T(8,128)(2,1)S(1)}, bf16[512,2048]{1,0:T(8,128)(2,1)S(1)}) custom-call(s32[8]{0:T(128)S(1)} %reshape.62.places_ref, bf16[128,2048]{1,0:T(8,128)(2,1)S(1)} %pad_maximum_fusion.refs_0_, bf16[128,2048]{1,0:T(8,128)(2,1)S(1)} %copy-done.14, bf16[128,2048]{1,0:T(8,128)(2,1)S(1)} %copy-done.25, ...), custom_call_target="tpu_custom_call" | custom-call | tf_op jit(solution)/shard_map/chunk_grads/pallas_call | solution.py:177
  197.3 3.8 %collective-permute-done.28 = bf16[512,2048]{1,0:T(8,128)(2,1)S(1)} collective-permute-done((bf16[512,2048]{1,0:T(8,128)(2,1)S(1)}, bf16[512,2048]{1,0:T(8,128)(2,1)S(1)}, u32[]{:S(2)}, u32[]{:S(2)}) %collective-permute-start.28) | collective-permute-done | bytes 2097184 | tf_op jit(solution)/shard_map/ppermute | solution.py:262
  201.1 1.7 add_convert_fusion
  204.0 3.2 %fusion.31 = (bf16[256,3584]{1,0:T(8,128)(2,1)}, bf16[256,3584]{1,0:T(8,128)(2,1)}) fusion(bf16[256,3584]{1,0:T(8,128)(2,1)} %copy-done.60, bf16[256,2048]{1,0:T(8,128)(2,1)} %collective-permute-done.27, bf16[512,2048]{1,0:T(8,128)(2,1)} %copy-done.57, bf16[512,2048]{1,0:T(8,128)(2,1)S(1)} %copy-done.38, bf16[256,3584]{1,0:T(8,128)(2,1)} %copy-done.59), kind=kLoop, calls=%fused_computation.54 | loop fusion | flops 3670016 | bytes 4194304 | tf_op jit(solution)/shard_map/dynamic_update_slice | solution.py:277
  207.2 7.5 %reduce-scatter.2.cloned.1.call-done = bf16[256,1024]{1,0:T(8,128)(2,1)} async-done(((bf16[1024,1024]{1,0:T(8,128)(2,1)}), bf16[256,1024]{1,0:T(8,128)(2,1)}) %reduce-scatter.2.cloned.1.call-update) | async-done | bytes 524304 | tf_op jit(solution)/shard_map/reduce_scatter | solution.py:279
  214.7 2.2 reverse_select_fusion
  216.9 10.5 %collective-permute-done.29 = bf16[256,2048]{1,0:T(8,128)(2,1)} collective-permute-done((bf16[256,2048]{1,0:T(8,128)(2,1)}, bf16[256,2048]{1,0:T(8,128)(2,1)}, u32[]{:S(2)}, u32[]{:S(2)}) %collective-permute-start.29) | collective-permute-done | bytes 1048608 | tf_op jit(solution)/shard_map/ppermute | solution.py:264
  227.4 3.5 %fusion.32 = (bf16[256,3584]{1,0:T(8,128)(2,1)}, bf16[256,3584]{1,0:T(8,128)(2,1)}) fusion(bf16[256,3584]{1,0:T(8,128)(2,1)} %get-tuple-element.153, bf16[256,2048]{1,0:T(8,128)(2,1)} %collective-permute-done.29, bf16[512,2048]{1,0:T(8,128)(2,1)} %copy-done.58, bf16[512,2048]{1,0:T(8,128)(2,1)} %copy-done.39, bf16[256,3584]{1,0:T(8,128)(2,1)} %get-tuple-element.154), kind=kLoop, calls=%fused_computation.55 | loop fusion | flops 3670016 | bytes 4194304 | tf_op jit(solution)/shard_map/dynamic_update_slice | solution.py:277
  (186 shorter events, 33.5 us)
Async XLA Ops:
  7.2 58.8 %all-gather.3.cloned.1.call-start = ((), (), s32[]{:S(2)}) async-start(), calls=%async_computation.1 | async-start | bytes 2621440 | tf_op jit(solution)/shard_map/all_gather | solution.py:209
  7.9 97.6 %all-gather.5.cloned.1.call-start = ((), (), s32[]{:S(2)}) async-start(), calls=%async_computation.2 | async-start | bytes 5242880 | tf_op jit(solution)/shard_map/all_gather | solution.py:202
  9.2 12.3 %collective-permute-start = (bf16[128,1024]{1,0:T(8,128)(2,1)S(1)}, bf16[128,1024]{1,0:T(8,128)(2,1)S(1)}, u32[]{:S(2)}, u32[]{:S(2)}) collective-permute-start(bf16[128,1024]{1,0:T(8,128)(2,1)S(1)} %pad_maximum_fusion.3.refs_0_), channel_id=1, source_target_pairs={{0,8},{4,12},{8,16},{12,20},{16,24},{20,28},{24,0},{28,4},{1,9},{5... | collective-permute-start | bytes 786440 | tf_op jit(solution)/shard_map/ppermute | solution.py:200
  11.4 10.1 %collective-permute-start.1 = (bf16[128,1024]{1,0:T(8,128)(2,1)S(1)}, bf16[128,1024]{1,0:T(8,128)(2,1)S(1)}, u32[]{:S(2)}, u32[]{:S(2)}) collective-permute-start(bf16[128,1024]{1,0:T(8,128)(2,1)S(1)} %pad_maximum_fusion.3.refs_0_), channel_id=1, source_target_pairs={{0,24},{4,28},{8,0},{12,4},{16,8},{20,12},{24,16},{28,20},{1,25},{... | collective-permute-start | bytes 786440 | tf_op jit(solution)/shard_map/ppermute | solution.py:201
  12.9 9.4 %collective-permute-start.2 = (bf16[128,1024]{1,0:T(8,128)(2,1)S(1)}, bf16[128,1024]{1,0:T(8,128)(2,1)S(1)}, u32[]{:S(2)}, u32[]{:S(2)}) collective-permute-start(bf16[128,1024]{1,0:T(8,128)(2,1)S(1)} %pad_maximum_fusion.3.refs_0_), channel_id=1, source_target_pairs={{0,4},{4,0},{8,12},{12,8},{16,20},{20,16},{24,28},{28,24},{1,5},{5... | collective-permute-start | bytes 786440 | tf_op jit(solution)/shard_map/ppermute | solution.py:199
  18.7 19.8 %collective-permute-start.5 = (bf16[128,2048]{1,0:T(8,128)(2,1)S(1)}, bf16[128,2048]{1,0:T(8,128)(2,1)S(1)}, u32[]{:S(2)}, u32[]{:S(2)}) collective-permute-start(bf16[128,2048]{1,0:T(8,128)(2,1)S(1)} %pad_maximum_fusion.2.refs_0_), channel_id=1, source_target_pairs={{0,8},{4,12},{8,16},{12,20},{16,24},{20,28},{24,0},{28,4},{1,9},{5... | collective-permute-start | bytes 1572872 | tf_op jit(solution)/shard_map/ppermute | solution.py:200
  18.8 19.7 %collective-permute-start.13 = (bf16[128,2048]{1,0:T(8,128)(2,1)S(1)}, bf16[128,2048]{1,0:T(8,128)(2,1)S(1)}, u32[]{:S(2)}, u32[]{:S(2)}) collective-permute-start(bf16[128,2048]{1,0:T(8,128)(2,1)S(1)} %pad_maximum_fusion.2.refs_0_), channel_id=1, source_target_pairs={{0,24},{4,28},{8,0},{12,4},{16,8},{20,12},{24,16},{28,20},{1,25},{... | collective-permute-start | bytes 1572872 | tf_op jit(solution)/shard_map/ppermute | solution.py:201
  22.2 17.1 %collective-permute-start.3 = (bf16[128,2048]{1,0:T(8,128)(2,1)S(1)}, bf16[128,2048]{1,0:T(8,128)(2,1)S(1)}, u32[]{:S(2)}, u32[]{:S(2)}) collective-permute-start(bf16[128,2048]{1,0:T(8,128)(2,1)S(1)} %pad_maximum_fusion.1.refs_0_), channel_id=1, source_target_pairs={{0,4},{4,0},{8,12},{12,8},{16,20},{20,16},{24,28},{28,24},{1,5},{5... | collective-permute-start | bytes 1572872 | tf_op jit(solution)/shard_map/ppermute | solution.py:199
  24.7 11.9 %collective-permute-start.11 = (bf16[128,1024]{1,0:T(8,128)(2,1)S(1)}, bf16[128,1024]{1,0:T(8,128)(2,1)S(1)}, u32[]{:S(2)}, u32[]{:S(2)}) collective-permute-start(bf16[128,1024]{1,0:T(8,128)(2,1)S(1)} %collective-permute-done.2.refs_1_), channel_id=1, source_target_pairs={{0,24},{4,28},{8,0},{12,4},{16,8},{20,12},{24,16},{28,20},{1,25},{... | collective-permute-start | bytes 786440 | tf_op jit(solution)/shard_map/ppermute | solution.py:201
  25.9 11.8 %collective-permute-start.14 = (bf16[128,1024]{1,0:T(8,128)(2,1)S(1)}, bf16[128,1024]{1,0:T(8,128)(2,1)S(1)}, u32[]{:S(2)}, u32[]{:S(2)}) collective-permute-start(bf16[128,1024]{1,0:T(8,128)(2,1)S(1)} %collective-permute-done.2.refs_1_), channel_id=1, source_target_pairs={{0,8},{4,12},{8,16},{12,20},{16,24},{20,28},{24,0},{28,4},{1,9},{5... | collective-permute-start | bytes 786440 | tf_op jit(solution)/shard_map/ppermute | solution.py:200
  41.0 173.7 %reduce-scatter.2.cloned.1.call-start = ((), (), s32[]{:S(2)}) async-start(), calls=%async_computation.3 | async-start | bytes 2621440 | tf_op jit(solution)/shard_map/reduce_scatter | solution.py:279
  41.1 12.8 %collective-permute-start.6 = (bf16[128,2048]{1,0:T(8,128)(2,1)S(1)}, bf16[128,2048]{1,0:T(8,128)(2,1)S(1)}, u32[]{:S(2)}, u32[]{:S(2)}) collective-permute-start(bf16[128,2048]{1,0:T(8,128)(2,1)S(1)} %pad_maximum_fusion.2.refs_0_), channel_id=1, source_target_pairs={{0,4},{4,0},{8,12},{12,8},{16,20},{20,16},{24,28},{28,24},{1,5},{5... | collective-permute-start | bytes 1572872 | tf_op jit(solution)/shard_map/ppermute | solution.py:199
  42.6 22.6 %collective-permute-start.4 = (bf16[128,2048]{1,0:T(8,128)(2,1)S(1)}, bf16[128,2048]{1,0:T(8,128)(2,1)S(1)}, u32[]{:S(2)}, u32[]{:S(2)}) collective-permute-start(bf16[128,2048]{1,0:T(8,128)(2,1)S(1)} %pad_maximum_fusion.refs_0_), channel_id=1, source_target_pairs={{0,4},{4,0},{8,12},{12,8},{16,20},{20,16},{24,28},{28,24},{1,5},{5... | collective-permute-start | bytes 1572872 | tf_op jit(solution)/shard_map/ppermute | solution.py:199
  44.2 6.7 %collective-permute-start.12 = (bf16[128,1024]{1,0:T(8,128)(2,1)S(1)}, bf16[128,1024]{1,0:T(8,128)(2,1)S(1)}, u32[]{:S(2)}, u32[]{:S(2)}) collective-permute-start(bf16[128,1024]{1,0:T(8,128)(2,1)S(1)} %collective-permute-done.refs_6_), channel_id=1, source_target_pairs={{0,8},{4,12},{8,16},{12,20},{16,24},{20,28},{24,0},{28,4},{1,9},{5... | collective-permute-start | bytes 786440 | tf_op jit(solution)/shard_map/ppermute | solution.py:200
  45.0 6.7 %collective-permute-start.15 = (bf16[128,1024]{1,0:T(8,128)(2,1)S(1)}, bf16[128,1024]{1,0:T(8,128)(2,1)S(1)}, u32[]{:S(2)}, u32[]{:S(2)}) collective-permute-start(bf16[128,1024]{1,0:T(8,128)(2,1)S(1)} %collective-permute-done.11.refs_3_), channel_id=1, source_target_pairs={{0,24},{4,28},{8,0},{12,4},{16,8},{20,12},{24,16},{28,20},{1,25},{... | collective-permute-start | bytes 786440 | tf_op jit(solution)/shard_map/ppermute | solution.py:201
  53.9 11.2 %copy-start.15 = (bf16[128,2048]{1,0:T(8,128)(2,1)}, bf16[128,2048]{1,0:T(8,128)(2,1)S(1)}, u32[]{:S(2)}) copy-start(bf16[128,2048]{1,0:T(8,128)(2,1)S(1)} %collective-permute-done.6.refs_1_) | copy-start | bytes 1572868
  72.4 5.6 %collective-permute-start.16 = (bf16[512,1024]{1,0:T(8,128)(2,1)S(1)}, bf16[512,1024]{1,0:T(8,128)(2,1)S(1)}, u32[]{:S(2)}, u32[]{:S(2)}) collective-permute-start(bf16[512,1024]{1,0:T(8,128)(2,1)S(1)} %get-tuple-element.97), channel_id=1, source_target_pairs={{0,32},{32,0},{64,96},{96,64},{1,33},{33,1},{65,97},{97,65},{2,34}... | collective-permute-start | bytes 3145736 | tf_op jit(solution)/shard_map/ppermute | solution.py:262
  75.7 25.2 %collective-permute-start.8 = (bf16[128,2048]{1,0:T(8,128)(2,1)S(1)}, bf16[128,2048]{1,0:T(8,128)(2,1)S(1)}, u32[]{:S(2)}, u32[]{:S(2)}) collective-permute-start(bf16[128,2048]{1,0:T(8,128)(2,1)S(1)} %copy-done.16), channel_id=1, source_target_pairs={{0,24},{4,28},{8,0},{12,4},{16,8},{20,12},{24,16},{28,20},{1,25},{... | collective-permute-start | bytes 1572872 | tf_op jit(solution)/shard_map/ppermute | solution.py:201
  78.1 26.2 %collective-permute-start.7 = (bf16[128,2048]{1,0:T(8,128)(2,1)S(1)}, bf16[128,2048]{1,0:T(8,128)(2,1)S(1)}, u32[]{:S(2)}, u32[]{:S(2)}) collective-permute-start(bf16[128,2048]{1,0:T(8,128)(2,1)S(1)} %copy-done.16), channel_id=1, source_target_pairs={{0,8},{4,12},{8,16},{12,20},{16,24},{20,28},{24,0},{28,4},{1,9},{5... | collective-permute-start | bytes 1572872 | tf_op jit(solution)/shard_map/ppermute | solution.py:200
  79.1 26.0 %collective-permute-start.23 = (bf16[256,1024]{1,0:T(8,128)(2,1)S(1)}, bf16[256,1024]{1,0:T(8,128)(2,1)}, u32[]{:S(2)}, u32[]{:S(2)}) collective-permute-start(bf16[256,1024]{1,0:T(8,128)(2,1)S(1)} %add_convert_fusion.3), channel_id=1, source_target_pairs={{0,64},{32,96},{64,0},{96,32},{1,65},{33,97},{65,1},{97,33},{2,66}... | collective-permute-start | bytes 1572872 | tf_op jit(solution)/shard_map/ppermute | solution.py:264
  107.7 23.7 %copy-start.2 = (bf16[1024,2048]{1,0:T(8,128)(2,1)S(1)}, bf16[1024,2048]{1,0:T(8,128)(2,1)}, u32[]{:S(2)}) copy-start(bf16[1024,2048]{1,0:T(8,128)(2,1)} %all-gather.5.cloned.1.call-done.refs_0_) | copy-start | bytes 12582916
  107.7 23.7 %copy-start.4 = (f32[1024,1024]{1,0:T(8,128)S(1)}, f32[1024,1024]{1,0:T(8,128)}, u32[]{:S(2)}) copy-start(f32[1024,1024]{1,0:T(8,128)} %copy-done.3) | copy-start | bytes 12582916
  113.4 15.5 %copy-start.13 = (bf16[128,2048]{1,0:T(8,128)(2,1)S(1)}, bf16[128,2048]{1,0:T(8,128)(2,1)}, u32[]{:S(2)}) copy-start(bf16[128,2048]{1,0:T(8,128)(2,1)} %copy-done.12) | copy-start | bytes 1572868
  113.4 4.5 %collective-permute-start.24 = (bf16[512,2048]{1,0:T(8,128)(2,1)S(1)}, bf16[512,2048]{1,0:T(8,128)(2,1)S(1)}, u32[]{:S(2)}, u32[]{:S(2)}) collective-permute-start(bf16[512,2048]{1,0:T(8,128)(2,1)S(1)} %get-tuple-element.111), channel_id=1, source_target_pairs={{0,32},{32,0},{64,96},{96,64},{1,33},{33,1},{65,97},{97,65},{2,34}... | collective-permute-start | bytes 6291464 | tf_op jit(solution)/shard_map/ppermute | solution.py:262
  114.1 14.7 %collective-permute-start.10 = (bf16[128,2048]{1,0:T(8,128)(2,1)S(1)}, bf16[128,2048]{1,0:T(8,128)(2,1)S(1)}, u32[]{:S(2)}, u32[]{:S(2)}) collective-permute-start(bf16[128,2048]{1,0:T(8,128)(2,1)S(1)} %pad_maximum_fusion.refs_0_), channel_id=1, source_target_pairs={{0,8},{4,12},{8,16},{12,20},{16,24},{20,28},{24,0},{28,4},{1,9},{5... | collective-permute-start | bytes 1572872 | tf_op jit(solution)/shard_map/ppermute | solution.py:200
  114.7 14.1 %collective-permute-start.17 = (bf16[128,2048]{1,0:T(8,128)(2,1)}, bf16[128,2048]{1,0:T(8,128)(2,1)S(1)}, u32[]{:S(2)}, u32[]{:S(2)}) collective-permute-start(bf16[128,2048]{1,0:T(8,128)(2,1)} %copy-done.20), channel_id=1, source_target_pairs={{0,24},{4,28},{8,0},{12,4},{16,8},{20,12},{24,16},{28,20},{1,25},{... | collective-permute-start | bytes 1572872 | tf_op jit(solution)/shard_map/ppermute | solution.py:201
  117.9 13.5 %copy-start.55 = (bf16[512,2048]{1,0:T(8,128)(2,1)}, bf16[512,2048]{1,0:T(8,128)(2,1)S(1)}, u32[]{:S(2)}) copy-start(bf16[512,2048]{1,0:T(8,128)(2,1)S(1)} %collective-permute-done.24) | copy-start | bytes 6291460
  118.3 33.0 %copy-start.11 = (bf16[128,2048]{1,0:T(8,128)(2,1)S(1)}, bf16[128,2048]{1,0:T(8,128)(2,1)}, u32[]{:S(2)}) copy-start(bf16[128,2048]{1,0:T(8,128)(2,1)} %copy-done.10) | copy-start | bytes 1572868
  118.3 33.0 %copy-start.17 = (bf16[128,2048]{1,0:T(8,128)(2,1)S(1)}, bf16[128,2048]{1,0:T(8,128)(2,1)}, u32[]{:S(2)}) copy-start(bf16[128,2048]{1,0:T(8,128)(2,1)} %copy-done.15) | copy-start | bytes 1572868
  118.3 33.0 %copy-start.21 = (bf16[128,2048]{1,0:T(8,128)(2,1)S(1)}, bf16[128,2048]{1,0:T(8,128)(2,1)}, u32[]{:S(2)}) copy-start(bf16[128,2048]{1,0:T(8,128)(2,1)} %copy-done.20) | copy-start | bytes 1572868
  118.3 33.0 %copy-start.23 = (bf16[128,2048]{1,0:T(8,128)(2,1)S(1)}, bf16[128,2048]{1,0:T(8,128)(2,1)}, u32[]{:S(2)}) copy-start(bf16[128,2048]{1,0:T(8,128)(2,1)} %copy-done.22) | copy-start | bytes 1572868
  118.4 33.0 %collective-permute-start.25 = (bf16[256,2048]{1,0:T(8,128)(2,1)S(1)}, bf16[256,2048]{1,0:T(8,128)(2,1)S(1)}, u32[]{:S(2)}, u32[]{:S(2)}) collective-permute-start(bf16[256,2048]{1,0:T(8,128)(2,1)S(1)} %add_convert_fusion.2), channel_id=1, source_target_pairs={{0,64},{32,96},{64,0},{96,32},{1,65},{33,97},{65,1},{97,33},{2,66}... | collective-permute-start | bytes 3145736 | tf_op jit(solution)/shard_map/ppermute | solution.py:264
  119.7 20.9 %collective-permute-start.22 = (bf16[128,2048]{1,0:T(8,128)(2,1)S(1)}, bf16[128,2048]{1,0:T(8,128)(2,1)S(1)}, u32[]{:S(2)}, u32[]{:S(2)}) collective-permute-start(bf16[128,2048]{1,0:T(8,128)(2,1)S(1)} %copy-done.9), channel_id=1, source_target_pairs={{0,8},{4,12},{8,16},{12,20},{16,24},{20,28},{24,0},{28,4},{1,9},{5... | collective-permute-start | bytes 1572872 | tf_op jit(solution)/shard_map/ppermute | solution.py:200
  120.3 20.3 %collective-permute-start.9 = (bf16[128,2048]{1,0:T(8,128)(2,1)S(1)}, bf16[128,2048]{1,0:T(8,128)(2,1)S(1)}, u32[]{:S(2)}, u32[]{:S(2)}) collective-permute-start(bf16[128,2048]{1,0:T(8,128)(2,1)S(1)} %pad_maximum_fusion.refs_0_), channel_id=1, source_target_pairs={{0,24},{4,28},{8,0},{12,4},{16,8},{20,12},{24,16},{28,20},{1,25},{... | collective-permute-start | bytes 1572872 | tf_op jit(solution)/shard_map/ppermute | solution.py:201
  128.8 44.5 %copy-start.18 = (bf16[128,2048]{1,0:T(8,128)(2,1)}, bf16[128,2048]{1,0:T(8,128)(2,1)S(1)}, u32[]{:S(2)}) copy-start(bf16[128,2048]{1,0:T(8,128)(2,1)S(1)} %collective-permute-done.10.refs_6_) | copy-start | bytes 1572868
  128.8 21.7 %collective-permute-start.18 = (bf16[128,2048]{1,0:T(8,128)(2,1)S(1)}, bf16[128,2048]{1,0:T(8,128)(2,1)S(1)}, u32[]{:S(2)}, u32[]{:S(2)}) collective-permute-start(bf16[128,2048]{1,0:T(8,128)(2,1)S(1)} %copy-done.13), channel_id=1, source_target_pairs={{0,24},{4,28},{8,0},{12,4},{16,8},{20,12},{24,16},{28,20},{1,25},{... | collective-permute-start | bytes 1572872 | tf_op jit(solution)/shard_map/ppermute | solution.py:201
  131.4 19.9 %collective-permute-start.21 = (bf16[128,2048]{1,0:T(8,128)(2,1)S(1)}, bf16[128,2048]{1,0:T(8,128)(2,1)S(1)}, u32[]{:S(2)}, u32[]{:S(2)}) collective-permute-start(bf16[128,2048]{1,0:T(8,128)(2,1)S(1)} %copy-done.13), channel_id=1, source_target_pairs={{0,8},{4,12},{8,16},{12,20},{16,24},{20,28},{24,0},{28,4},{1,9},{5... | collective-permute-start | bytes 1572872 | tf_op jit(solution)/shard_map/ppermute | solution.py:200
  140.6 32.8 %copy-start.24 = (bf16[128,2048]{1,0:T(8,128)(2,1)}, bf16[128,2048]{1,0:T(8,128)(2,1)S(1)}, u32[]{:S(2)}) copy-start(bf16[128,2048]{1,0:T(8,128)(2,1)S(1)} %collective-permute-done.9.refs_2_) | copy-start | bytes 1572868
  150.6 22.8 %copy-start.26 = (bf16[128,2048]{1,0:T(8,128)(2,1)}, bf16[128,2048]{1,0:T(8,128)(2,1)S(1)}, u32[]{:S(2)}) copy-start(bf16[128,2048]{1,0:T(8,128)(2,1)S(1)} %collective-permute-done.18.refs_3_) | copy-start | bytes 1572868
  151.3 22.1 %copy-start.28 = (bf16[128,2048]{1,0:T(8,128)(2,1)}, bf16[128,2048]{1,0:T(8,128)(2,1)S(1)}, u32[]{:S(2)}) copy-start(bf16[128,2048]{1,0:T(8,128)(2,1)S(1)} %collective-permute-done.21.refs_7_) | copy-start | bytes 1572868
  151.4 13.7 %copy-start.6 = (f32[1024,1024]{1,0:T(8,128)S(1)}, f32[1024,1024]{1,0:T(8,128)}, u32[]{:S(2)}) copy-start(f32[1024,1024]{1,0:T(8,128)} %copy-done.5) | copy-start | bytes 12582916
  157.3 15.1 %copy-start.37 = (bf16[512,2048]{1,0:T(8,128)(2,1)}, bf16[512,2048]{1,0:T(8,128)(2,1)S(1)}, u32[]{:S(2)}) copy-start(bf16[512,2048]{1,0:T(8,128)(2,1)S(1)} %get-tuple-element.121) | copy-start | bytes 6291460
  157.3 4.7 %collective-permute-start.26 = (bf16[512,2048]{1,0:T(8,128)(2,1)S(1)}, bf16[512,2048]{1,0:T(8,128)(2,1)S(1)}, u32[]{:S(2)}, u32[]{:S(2)}) collective-permute-start(bf16[512,2048]{1,0:T(8,128)(2,1)S(1)} %get-tuple-element.122), channel_id=1, source_target_pairs={{0,32},{32,0},{64,96},{96,64},{1,33},{33,1},{65,97},{97,65},{2,34}... | collective-permute-start | bytes 6291464 | tf_op jit(solution)/shard_map/ppermute | solution.py:262
  158.3 15.1 %collective-permute-start.19 = (bf16[128,2048]{1,0:T(8,128)(2,1)S(1)}, bf16[128,2048]{1,0:T(8,128)(2,1)S(1)}, u32[]{:S(2)}, u32[]{:S(2)}) collective-permute-start(bf16[128,2048]{1,0:T(8,128)(2,1)S(1)} %collective-permute-done.10.refs_6_), channel_id=1, source_target_pairs={{0,8},{4,12},{8,16},{12,20},{16,24},{20,28},{24,0},{28,4},{1,9},{5... | collective-permute-start | bytes 1572872 | tf_op jit(solution)/shard_map/ppermute | solution.py:200
  158.8 14.5 %collective-permute-start.20 = (bf16[128,2048]{1,0:T(8,128)(2,1)S(1)}, bf16[128,2048]{1,0:T(8,128)(2,1)S(1)}, u32[]{:S(2)}, u32[]{:S(2)}) collective-permute-start(bf16[128,2048]{1,0:T(8,128)(2,1)S(1)} %collective-permute-done.18.refs_3_), channel_id=1, source_target_pairs={{0,24},{4,28},{8,0},{12,4},{16,8},{20,12},{24,16},{28,20},{1,25},{... | collective-permute-start | bytes 1572872 | tf_op jit(solution)/shard_map/ppermute | solution.py:201
  163.7 24.7 %collective-permute-start.27 = (bf16[256,2048]{1,0:T(8,128)(2,1)}, bf16[256,2048]{1,0:T(8,128)(2,1)}, u32[]{:S(2)}, u32[]{:S(2)}) collective-permute-start(bf16[256,2048]{1,0:T(8,128)(2,1)} %add_convert_fusion.1), channel_id=1, source_target_pairs={{0,64},{32,96},{64,0},{96,32},{1,65},{33,97},{65,1},{97,33},{2,66}... | collective-permute-start | bytes 3145736 | tf_op jit(solution)/shard_map/ppermute | solution.py:264
  196.5 4.6 %collective-permute-start.28 = (bf16[512,2048]{1,0:T(8,128)(2,1)S(1)}, bf16[512,2048]{1,0:T(8,128)(2,1)S(1)}, u32[]{:S(2)}, u32[]{:S(2)}) collective-permute-start(bf16[512,2048]{1,0:T(8,128)(2,1)S(1)} %get-tuple-element.150), channel_id=1, source_target_pairs={{0,32},{32,0},{64,96},{96,64},{1,33},{33,1},{65,97},{97,65},{2,34}... | collective-permute-start | bytes 6291464 | tf_op jit(solution)/shard_map/ppermute | solution.py:262
  202.7 24.7 %collective-permute-start.29 = (bf16[256,2048]{1,0:T(8,128)(2,1)}, bf16[256,2048]{1,0:T(8,128)(2,1)}, u32[]{:S(2)}, u32[]{:S(2)}) collective-permute-start(bf16[256,2048]{1,0:T(8,128)(2,1)} %add_convert_fusion), channel_id=1, source_target_pairs={{0,64},{32,96},{64,0},{96,32},{1,65},{33,97},{65,1},{97,33},{2,66}... | collective-permute-start | bytes 3145736 | tf_op jit(solution)/shard_map/ppermute | solution.py:264
  (51 other events, 135.4 us)
Sparse Core Ops, SparseCore 0:
  9.7 34.0 all-gather.2
  46.0 59.5 all-gather.4
  183.7 30.9 reduce-scatter.1

commit v3 on v2

--- a/solution.py
+++ b/solution.py
@@ -111,7 +111,6 @@
     width = (input_columns if gate_weight is None else gate_weight).shape[0]
     w = hidden // 2
     tile = width // TILES
-    half = TILES // 2
     column = start // w
     with_weight, with_input = input_columns is not None, gate_weight is not None
 
@@ -122,7 +121,7 @@
         input_refs = take(1) if with_weight else []
         weight_refs = take(2) if with_input else []
         total_refs = take(1) if total is not None else []
-        part_refs = take(2) if with_weight else []
+        part_refs = take(3) if with_weight else []
         sum_refs = take(1) if with_input else []
         if count > 1:
             rows_ref = refs.pop(0)
@@ -137,13 +136,14 @@
         if with_weight:
             part = jnp.dot(input_refs[0][...], rows_ref[...], preferred_element_type=jnp.float32).astype(jnp.bfloat16)
 
-            @pl.when(pl.program_id(0) < half)
+            @pl.when(pl.program_id(0) == 0)
             def _():
-                part_refs[0][...] = part
-
-            @pl.when(pl.program_id(0) >= half)
+                part_refs[0][...] = part[: tile // 2]
+                part_refs[1][...] = part[tile // 2 :]
+
+            @pl.when(pl.program_id(0) == 1)
             def _():
-                part_refs[1][...] = part
+                part_refs[2][...] = part
 
         if with_input:
             across = (((1,), (1,)), ((), ()))
@@ -161,11 +161,9 @@
     if with_weight:
         in_specs.append(pl.BlockSpec((tile, tokens), lambda i, _: (i, 0)))
         operands.append(input_columns)
-        out_shape += [jax.ShapeDtypeStruct((width // 2, hidden), jnp.bfloat16)] * 2
-        out_specs += [
-            pl.BlockSpec((tile, hidden), lambda i, _: (jnp.minimum(i, half - 1), 0)),
-            pl.BlockSpec((tile, hidden), lambda i, _: (jnp.maximum(i - half, 0), 0)),
-        ]
+        for part_rows in (tile // 2, tile // 2, tile):
+            out_shape.append(jax.ShapeDtypeStruct((part_rows, hidden), jnp.bfloat16))
+            out_specs.append(pl.BlockSpec((part_rows, hidden), lambda i, _: (0, 0)))
     if with_input:
         in_specs += [pl.BlockSpec((tile, w), lambda i, _: (i, column))] * 2
         operands += [gate_weight, up_weight]
@@ -258,16 +256,17 @@
             gate_out, up_out = after_all([gate_out, up_out], total)
             earlier += [input_part, gate_out, up_out]
         pieces = after_all(pieces, *earlier)
-        send, keep = chunk_grads(places, pieces, input_columns, None, None, s, None, False)
-        core_part = lax.ppermute(send, "dp", CORE_SWAP)
-        chip_send[c] = (keep[:quarter].astype(jnp.float32) + core_part[:quarter].astype(jnp.float32)).astype(jnp.bfloat16)
+        send_pass, send_stay, keep = chunk_grads(places, pieces, input_columns, None, None, s, None, False)
+        core_pass = lax.ppermute(send_pass, "dp", CORE_SWAP)
+        core_stay = lax.ppermute(send_stay, "dp", CORE_SWAP)
+        chip_send[c] = (keep[:quarter].astype(jnp.float32) + core_pass.astype(jnp.float32)).astype(jnp.bfloat16)
         pair_part = pair_parts[c] = lax.ppermute(chip_send[c], "dp", PAIR_SWAP)
         if c < count - 1:
             pieces = after_all(pieces, chip_send[c])
             (total,) = chunk_grads(places, pieces, None, gate_weight, up_weight, s, total, False)
 
-        def finish(columns, keep=keep, core_part=core_part, pair_part=pair_part):
-            value = keep[quarter:, columns].astype(jnp.float32) + core_part[quarter:, columns].astype(jnp.float32)
+        def finish(columns, keep=keep, core_stay=core_stay, pair_part=pair_part):
+            value = keep[quarter:, columns].astype(jnp.float32) + core_stay[:, columns].astype(jnp.float32)
             return ((value + pair_part[:, columns].astype(jnp.float32)) * inverse_groups).astype(jnp.bfloat16)
 
         finishes[c] = finish

time: 238 us -> 261 us (1.097)
  waiting for transfers between devices: 84.1 us -> 105 us
  Pallas kernels: 50.2 us -> 53.2 us
    ppermute x4, waiting for transfers between devices: 10.7 us -> 38.4 us  [body(): pair_part = pair_parts[c] = lax.ppermute(chip_send[c], 'dp', PAIR_SWAP)]
    reduce_scatter x1, waiting for transfers between devices: 7.54 us -> 0.01 us  [body(): lax.psum_scatter(input_part, 'col', scatter_dimension=0, tiled=True)]
    ppermute x9, waiting for transfers between devices: 15.1 us -> 18.3 us  [body(): up = lambda value: lax.ppermute(value, 'row', ROW_UP)]
    ppermute x4 -> x8, waiting for transfers between devices: 5.76 us -> 2.66 us  [the longest x4 2.35 us: body(): core_pass = lax.ppermute(send_pass, 'dp', CORE_SWAP)]
    pallas_call x8, Pallas kernels: 47.4 us -> 50.4 us  [chunk_grads(): pl.pallas_call(kernel, out_shape=tuple(out_shape), grid_spec=pltpu.Prefet...]
    unnamed x132 -> x130, local copies, waits for them, and re-layouts: 26.4 us -> 24.1 us
    ppermute x4 -> x8, starting transfers between devices: 5.69 us -> 7.16 us  [the longest x4 5.51 us: body(): core_pass = lax.ppermute(send_pass, 'dp', CORE_SWAP)]
  transfers between devices with their start and end apart: 33 -> 37, of which waited for: 18 -> 16; matrix products, arithmetic and copies ran while one was open for 7% -> 7% of each run, Pallas kernels for 16% -> 15%
where the time goes in v3:
time: 261 us
  waiting for transfers between devices  105 us (40%)
  Pallas kernels  53.2 us (20%)
  starting transfers between devices  45 us (17%)
  local copies, waits for them, and re-layouts  24.4 us (9%)
  other arithmetic  18.9 us (7%)
  between operations  14.4 us (6%)
    pallas_call x8, Pallas kernels, chunk_grads(): pl.pallas_call(kernel, out_shape=tuple(out_shape), grid_spec=pltpu.Prefet...  50.4 us
    ppermute x4, waiting for transfers between devices, body(): pair_part = pair_parts[c] = lax.ppermute(chip_send[c], 'dp', PAIR_SWAP)  38.4 us
    ppermute x9, waiting for transfers between devices, body(): down = lambda value: lax.ppermute(value, 'row', ROW_DOWN)  31.5 us
    unnamed x130, local copies, waits for them, and re-layouts  24.1 us
    ppermute x9, starting transfers between devices, body(): down = lambda value: lax.ppermute(value, 'row', ROW_DOWN)  20.1 us
    ppermute x9, waiting for transfers between devices, body(): up = lambda value: lax.ppermute(value, 'row', ROW_UP)  18.3 us
    ppermute x4, waiting for transfers between devices, body(): swap = lambda value: lax.ppermute(value, 'row', ROW_SWAP)  12.8 us
    ppermute x4, starting transfers between devices, body(): swap = lambda value: lax.ppermute(value, 'row', ROW_SWAP)  9.11 us
  transfers between devices with their start and end apart: 37, of which 16 were waited for; matrix products, arithmetic and copies ran while one was open for 7% of the time, Pallas kernels for 15%

profile of v3, /device:TPU:1, one launch (start us, length us, event | category | flops | bytes accessed | tf_op | source)
XLA Modules:
  0.0 260.8 jit_solution(17769336705895999838)
XLA Ops:
  9.2 2.2 collective-permute-start
  11.4 1.5 collective-permute-start.1
  12.9 3.6 %collective-permute-start.2 = (bf16[128,1024]{1,0:T(8,128)(2,1)S(1)}, bf16[128,1024]{1,0:T(8,128)(2,1)S(1)}, u32[]{:S(2)}, u32[]{:S(2)}) collective-permute-start(bf16[128,1024]{1,0:T(8,128)(2,1)S(1)} %pad_maximum_fusion.3.refs_0_), channel_id=1, source_target_pairs={{0,4},{4,0},{8,12},{12,8},{16,20},{20,16},{24,28},{28,24},{1,5},{5... | collective-permute-start | bytes 786440 | tf_op jit(solution)/shard_map/ppermute | solution.py:197
  16.5 2.2 fusion.8
  18.8 2.7 %collective-permute-start.13 = (bf16[128,2048]{1,0:T(8,128)(2,1)S(1)}, bf16[128,2048]{1,0:T(8,128)(2,1)S(1)}, u32[]{:S(2)}, u32[]{:S(2)}) collective-permute-start(bf16[128,2048]{1,0:T(8,128)(2,1)S(1)} %pad_maximum_fusion.2.refs_0_), channel_id=1, source_target_pairs={{0,24},{4,28},{8,0},{12,4},{16,8},{20,12},{24,16},{28,20},{1,25},{... | collective-permute-start | bytes 1572872 | tf_op jit(solution)/shard_map/ppermute | solution.py:199
  22.2 2.5 collective-permute-start.3
  26.9 9.8 %collective-permute-done.11.refs_3_ = bf16[128,1024]{1,0:T(8,128)(2,1)S(1)} collective-permute-done((bf16[128,1024]{1,0:T(8,128)(2,1)S(1)}, bf16[128,1024]{1,0:T(8,128)(2,1)S(1)}, u32[]{:S(2)}, u32[]{:S(2)}) %collective-permute-start.11) | collective-permute-done | bytes 262176 | tf_op jit(solution)/shard_map/ppermute | solution.py:199
  39.3 1.6 join_rows.1
  41.1 1.5 collective-permute-start.6
  42.6 1.6 collective-permute-start.4
  45.0 2.7 %collective-permute-start.15 = (bf16[128,1024]{1,0:T(8,128)(2,1)S(1)}, bf16[128,1024]{1,0:T(8,128)(2,1)S(1)}, u32[]{:S(2)}, u32[]{:S(2)}) collective-permute-start(bf16[128,1024]{1,0:T(8,128)(2,1)S(1)} %collective-permute-done.11.refs_3_), channel_id=1, source_target_pairs={{0,24},{4,28},{8,0},{12,4},{16,8},{20,12},{24,16},{28,20},{1,25},{... | collective-permute-start | bytes 786440 | tf_op jit(solution)/shard_map/ppermute | solution.py:199
  48.5 2.5 collective-permute-done.12.refs_4_
  52.4 1.5 collective-permute-done.6.refs_1_
  53.9 11.2 %collective-permute-done.4.refs_1_ = bf16[128,2048]{1,0:T(8,128)(2,1)S(1)} collective-permute-done((bf16[128,2048]{1,0:T(8,128)(2,1)S(1)}, bf16[128,2048]{1,0:T(8,128)(2,1)S(1)}, u32[]{:S(2)}, u32[]{:S(2)}) %collective-permute-start.4) | collective-permute-done | bytes 524320 | tf_op jit(solution)/shard_map/ppermute | solution.py:197
  66.0 1.6 copy-done.34
  69.0 3.4 %chunk_grads.8 = (bf16[256,1024]{1,0:T(8,128)(2,1)S(1)}, bf16[256,1024]{1,0:T(8,128)(2,1)S(1)}, bf16[512,1024]{1,0:T(8,128)(2,1)S(1)}) custom-call(s32[8]{0:T(128)S(1)} %reshape.62.places_ref, bf16[128,1024]{1,0:T(8,128)(2,1)S(1)} %pad_maximum_fusion.3.refs_0_, bf16[128,1024]{1,0:T(8,128)(2,1)S(1)} %copy-done.46, bf16[128,1024]{1,0:T(8,128)(2,1)S(1)} %copy-done.44, ...), custom_call_target="tpu_custom_call" | custom-call | tf_op jit(solution)/shard_map/chunk_grads/pallas_call | solution.py:175
  72.5 3.2 %collective-permute-start.16 = (bf16[256,1024]{1,0:T(8,128)(2,1)S(1)}, bf16[256,1024]{1,0:T(8,128)(2,1)S(1)}, u32[]{:S(2)}, u32[]{:S(2)}) collective-permute-start(bf16[256,1024]{1,0:T(8,128)(2,1)S(1)} %get-tuple-element.101), channel_id=1, source_target_pairs={{0,32},{32,0},{64,96},{96,64},{1,33},{33,1},{65,97},{97,65},{2,34}... | collective-permute-start | bytes 1572872 | tf_op jit(solution)/shard_map/ppermute | solution.py:260
  75.7 2.4 collective-permute-start.8
  79.3 3.2 %copy-done = bf16[1024,3584]{1,0:T(8,128)(2,1)S(1)} copy-done((bf16[1024,3584]{1,0:T(8,128)(2,1)S(1)}, bf16[1024,3584]{1,0:T(8,128)(2,1)}, u32[]{:S(2)}) %copy-start) | copy-done | bytes 7340056
  82.5 4.6 %chunk_grads.9.refs_3_ = f32[1024,1024]{1,0:T(8,128)S(1)} custom-call(s32[8]{0:T(128)S(1)} %reshape.62.places_ref, bf16[128,1024]{1,0:T(8,128)(2,1)S(1)} %pad_maximum_fusion.3.refs_0_, bf16[128,1024]{1,0:T(8,128)(2,1)S(1)} %copy-done.46, bf16[128,1024]{1,0:T(8,128)(2,1)S(1)} %copy-done.44, bf16[128,1024]{1,0:T(8,128)(2,1)S(1)} %copy-done.48, ...), custom_call_target="tpu_custom_call" | custom-call | tf_op jit(solution)/shard_map/chunk_grads/pallas_call | solution.py:175
  87.1 2.0 copy-done.3
  89.1 11.7 %collective-permute-done.8.refs_3_ = bf16[128,2048]{1,0:T(8,128)(2,1)S(1)} collective-permute-done((bf16[128,2048]{1,0:T(8,128)(2,1)S(1)}, bf16[128,2048]{1,0:T(8,128)(2,1)S(1)}, u32[]{:S(2)}, u32[]{:S(2)}) %collective-permute-start.8) | collective-permute-done | bytes 524320 | tf_op jit(solution)/shard_map/ppermute | solution.py:199
  100.9 3.4 %collective-permute-done.7.refs_7_ = bf16[128,2048]{1,0:T(8,128)(2,1)S(1)} collective-permute-done((bf16[128,2048]{1,0:T(8,128)(2,1)S(1)}, bf16[128,2048]{1,0:T(8,128)(2,1)S(1)}, u32[]{:S(2)}, u32[]{:S(2)}) %collective-permute-start.7) | collective-permute-done | bytes 524320 | tf_op jit(solution)/shard_map/ppermute | solution.py:198
  105.5 2.2 copy-done.1
  107.7 6.6 %chunk_grads.10 = (bf16[256,2048]{1,0:T(8,128)(2,1)S(1)}, bf16[256,2048]{1,0:T(8,128)(2,1)}, bf16[512,2048]{1,0:T(8,128)(2,1)S(1)}) custom-call(s32[8]{0:T(128)S(1)} %reshape.62.places_ref, bf16[1024,2048]{1,0:T(8,128)(2,1)S(1)} %copy-done.1, bf16[1024,1024]{1,0:T(8,128)(2,1)S(1)} %order_input.1.refs_8_.refs_1_), custom_call_target="tpu_custom_call" | custom-call | tf_op jit(solution)/shard_map/chunk_grads/pallas_call | solution.py:175
  115.6 2.1 collective-permute-start.17
  119.7 2.5 collective-permute-start.9
  122.2 7.6 %collective-permute-done.10.refs_6_ = bf16[128,2048]{1,0:T(8,128)(2,1)S(1)} collective-permute-done((bf16[128,2048]{1,0:T(8,128)(2,1)S(1)}, bf16[128,2048]{1,0:T(8,128)(2,1)S(1)}, u32[]{:S(2)}, u32[]{:S(2)}) %collective-permute-start.10) | collective-permute-done | bytes 524320 | tf_op jit(solution)/shard_map/ppermute | solution.py:198
  129.8 2.6 collective-permute-start.18
  132.3 7.1 %chunk_grads.11.refs_10_ = f32[1024,1024]{1,0:T(8,128)S(1)} custom-call(s32[8]{0:T(128)S(1)} %reshape.62.places_ref, bf16[1024,2048]{1,0:T(8,128)(2,1)S(1)} %copy-done.2, bf16[1024,3584]{1,0:T(8,128)(2,1)} %refs_8_.5, bf16[1024,3584]{1,0:T(8,128)(2,1)} %refs_9_.5, f32[1024,1024]{1,0:T(8,128)S(1)} %copy-done.4), custom_call_target="tpu_custom_call" | custom-call | tf_op jit(solution)/shard_map/chunk_grads/pallas_call | solution.py:175
  139.5 2.0 copy-done.5
  141.5 9.9 %collective-permute-done.18.refs_3_ = bf16[128,2048]{1,0:T(8,128)(2,1)S(1)} collective-permute-done((bf16[128,2048]{1,0:T(8,128)(2,1)S(1)}, bf16[128,2048]{1,0:T(8,128)(2,1)S(1)}, u32[]{:S(2)}, u32[]{:S(2)}) %collective-permute-start.18) | collective-permute-done | bytes 524320 | tf_op jit(solution)/shard_map/ppermute | solution.py:199
  152.3 7.0 %chunk_grads.12 = (bf16[256,2048]{1,0:T(8,128)(2,1)S(1)}, bf16[256,2048]{1,0:T(8,128)(2,1)}, bf16[512,2048]{1,0:T(8,128)(2,1)S(1)}) custom-call(s32[8]{0:T(128)S(1)} %reshape.62.places_ref, bf16[128,2048]{1,0:T(8,128)(2,1)S(1)} %pad_maximum_fusion.2.refs_0_, bf16[128,2048]{1,0:T(8,128)(2,1)S(1)} %copy-done.17, bf16[128,2048]{1,0:T(8,128)(2,1)S(1)} %copy-done.11, ...), custom_call_target="tpu_custom_call" | custom-call | tf_op jit(solution)/shard_map/chunk_grads/pallas_call | solution.py:175
  160.6 2.4 collective-permute-start.20
  163.5 1.4 add_convert_fusion.1
  164.8 7.4 %chunk_grads.13.refs_10_ = f32[1024,1024]{1,0:T(8,128)S(1)} custom-call(s32[8]{0:T(128)S(1)} %reshape.62.places_ref, bf16[128,2048]{1,0:T(8,128)(2,1)S(1)} %pad_maximum_fusion.2.refs_0_, bf16[128,2048]{1,0:T(8,128)(2,1)S(1)} %copy-done.17, bf16[128,2048]{1,0:T(8,128)(2,1)S(1)} %copy-done.11, bf16[128,2048]{1,0:T(8,128)(2,1)S(1)} %copy-done.23, ...), custom_call_target="tpu_custom_call" | custom-call | tf_op jit(solution)/shard_map/chunk_grads/pallas_call | solution.py:175
  172.3 2.9 %collective-permute-done.19.refs_4_ = bf16[128,2048]{1,0:T(8,128)(2,1)S(1)} collective-permute-done((bf16[128,2048]{1,0:T(8,128)(2,1)S(1)}, bf16[128,2048]{1,0:T(8,128)(2,1)S(1)}, u32[]{:S(2)}, u32[]{:S(2)}) %collective-permute-start.19) | collective-permute-done | bytes 524320 | tf_op jit(solution)/shard_map/ppermute | solution.py:198
  175.2 7.3 %chunk_grads.14 = bf16[1024,1024]{1,0:T(8,128)(2,1)S(1)} custom-call(s32[8]{0:T(128)S(1)} %reshape.62.places_ref, bf16[128,2048]{1,0:T(8,128)(2,1)S(1)} %pad_maximum_fusion.refs_0_, bf16[128,2048]{1,0:T(8,128)(2,1)S(1)} %copy-done.13, bf16[128,2048]{1,0:T(8,128)(2,1)S(1)} %collective-permute-done.9.refs_2_, ...), custom_call_target="tpu_custom_call" | custom-call | tf_op jit(solution)/shard_map/chunk_grads/pallas_call | solution.py:175
  188.7 1.4 multiply_convert_fusion.6
  192.0 2.0 fusion.28
  194.0 18.3 %collective-permute-done.30 = bf16[256,2048]{1,0:T(8,128)(2,1)S(1)} collective-permute-done((bf16[256,2048]{1,0:T(8,128)(2,1)}, bf16[256,2048]{1,0:T(8,128)(2,1)S(1)}, u32[]{:S(2)}, u32[]{:S(2)}) %collective-permute-start.30) | collective-permute-done | bytes 1048608 | tf_op jit(solution)/shard_map/ppermute | solution.py:263
  212.3 6.9 %chunk_grads.15 = (bf16[256,2048]{1,0:T(8,128)(2,1)S(1)}, bf16[256,2048]{1,0:T(8,128)(2,1)}, bf16[512,2048]{1,0:T(8,128)(2,1)S(1)}) custom-call(s32[8]{0:T(128)S(1)} %reshape.62.places_ref, bf16[128,2048]{1,0:T(8,128)(2,1)S(1)} %pad_maximum_fusion.refs_0_, bf16[128,2048]{1,0:T(8,128)(2,1)S(1)} %copy-done.14, bf16[128,2048]{1,0:T(8,128)(2,1)S(1)} %copy-done.21, ...), custom_call_target="tpu_custom_call" | custom-call | tf_op jit(solution)/shard_map/chunk_grads/pallas_call | solution.py:175
  220.5 2.3 collective-permute-done.32
  222.9 1.4 add_convert_fusion
  225.5 3.3 %fusion.31 = (bf16[256,3584]{1,0:T(8,128)(2,1)}, bf16[256,3584]{1,0:T(8,128)(2,1)}) fusion(bf16[256,3584]{1,0:T(8,128)(2,1)} %copy-done.59, bf16[256,2048]{1,0:T(8,128)(2,1)} %copy-done.62, bf16[256,2048]{1,0:T(8,128)(2,1)} %collective-permute-done.29, bf16[512,2048]{1,0:T(8,128)(2,1)S(1)} %copy-done.38, bf16[256,3584]{1,0:T(8,128)(2,1)} %copy-done.58), kind=kLoop, calls=%fused_computation.54 | loop fusion | flops 3670016 | bytes 4194304 | tf_op jit(solution)/shard_map/dynamic_update_slice | solution.py:276
  228.8 20.2 %collective-permute-done.33 = bf16[256,2048]{1,0:T(8,128)(2,1)} collective-permute-done((bf16[256,2048]{1,0:T(8,128)(2,1)}, bf16[256,2048]{1,0:T(8,128)(2,1)}, u32[]{:S(2)}, u32[]{:S(2)}) %collective-permute-start.33) | collective-permute-done | bytes 1048608 | tf_op jit(solution)/shard_map/ppermute | solution.py:263
  248.9 3.1 %fusion.32 = (bf16[256,3584]{1,0:T(8,128)(2,1)}, bf16[256,3584]{1,0:T(8,128)(2,1)}) fusion(bf16[256,3584]{1,0:T(8,128)(2,1)} %get-tuple-element.161, bf16[256,2048]{1,0:T(8,128)(2,1)} %collective-permute-done.33, bf16[256,2048]{1,0:T(8,128)(2,1)} %collective-permute-done.31, bf16[512,2048]{1,0:T(8,128)(2,1)S(1)} %copy-done.40, ...), kind=kLoop, calls=%fused_computation.55 | loop fusion | flops 3670016 | bytes 4194304 | tf_op jit(solution)/shard_map/dynamic_update_slice | solution.py:276
  252.1 2.2 reverse_select_fusion
  (192 shorter events, 31.6 us)
Async XLA Ops:
  7.2 58.8 %all-gather.3.cloned.1.call-start = ((), (), s32[]{:S(2)}) async-start(), calls=%async_computation.1 | async-start | bytes 2621440 | tf_op jit(solution)/shard_map/all_gather | solution.py:207
  7.9 97.6 %all-gather.5.cloned.1.call-start = ((), (), s32[]{:S(2)}) async-start(), calls=%async_computation.2 | async-start | bytes 5242880 | tf_op jit(solution)/shard_map/all_gather | solution.py:200
  9.2 12.3 %collective-permute-start = (bf16[128,1024]{1,0:T(8,128)(2,1)S(1)}, bf16[128,1024]{1,0:T(8,128)(2,1)S(1)}, u32[]{:S(2)}, u32[]{:S(2)}) collective-permute-start(bf16[128,1024]{1,0:T(8,128)(2,1)S(1)} %pad_maximum_fusion.3.refs_0_), channel_id=1, source_target_pairs={{0,8},{4,12},{8,16},{12,20},{16,24},{20,28},{24,0},{28,4},{1,9},{5... | collective-permute-start | bytes 786440 | tf_op jit(solution)/shard_map/ppermute | solution.py:198
  11.4 10.2 %collective-permute-start.1 = (bf16[128,1024]{1,0:T(8,128)(2,1)S(1)}, bf16[128,1024]{1,0:T(8,128)(2,1)S(1)}, u32[]{:S(2)}, u32[]{:S(2)}) collective-permute-start(bf16[128,1024]{1,0:T(8,128)(2,1)S(1)} %pad_maximum_fusion.3.refs_0_), channel_id=1, source_target_pairs={{0,24},{4,28},{8,0},{12,4},{16,8},{20,12},{24,16},{28,20},{1,25},{... | collective-permute-start | bytes 786440 | tf_op jit(solution)/shard_map/ppermute | solution.py:199
  12.9 9.3 %collective-permute-start.2 = (bf16[128,1024]{1,0:T(8,128)(2,1)S(1)}, bf16[128,1024]{1,0:T(8,128)(2,1)S(1)}, u32[]{:S(2)}, u32[]{:S(2)}) collective-permute-start(bf16[128,1024]{1,0:T(8,128)(2,1)S(1)} %pad_maximum_fusion.3.refs_0_), channel_id=1, source_target_pairs={{0,4},{4,0},{8,12},{12,8},{16,20},{20,16},{24,28},{28,24},{1,5},{5... | collective-permute-start | bytes 786440 | tf_op jit(solution)/shard_map/ppermute | solution.py:197
  18.7 19.8 %collective-permute-start.5 = (bf16[128,2048]{1,0:T(8,128)(2,1)S(1)}, bf16[128,2048]{1,0:T(8,128)(2,1)S(1)}, u32[]{:S(2)}, u32[]{:S(2)}) collective-permute-start(bf16[128,2048]{1,0:T(8,128)(2,1)S(1)} %pad_maximum_fusion.2.refs_0_), channel_id=1, source_target_pairs={{0,8},{4,12},{8,16},{12,20},{16,24},{20,28},{24,0},{28,4},{1,9},{5... | collective-permute-start | bytes 1572872 | tf_op jit(solution)/shard_map/ppermute | solution.py:198
  18.8 19.7 %collective-permute-start.13 = (bf16[128,2048]{1,0:T(8,128)(2,1)S(1)}, bf16[128,2048]{1,0:T(8,128)(2,1)S(1)}, u32[]{:S(2)}, u32[]{:S(2)}) collective-permute-start(bf16[128,2048]{1,0:T(8,128)(2,1)S(1)} %pad_maximum_fusion.2.refs_0_), channel_id=1, source_target_pairs={{0,24},{4,28},{8,0},{12,4},{16,8},{20,12},{24,16},{28,20},{1,25},{... | collective-permute-start | bytes 1572872 | tf_op jit(solution)/shard_map/ppermute | solution.py:199
  22.2 17.1 %collective-permute-start.3 = (bf16[128,2048]{1,0:T(8,128)(2,1)S(1)}, bf16[128,2048]{1,0:T(8,128)(2,1)S(1)}, u32[]{:S(2)}, u32[]{:S(2)}) collective-permute-start(bf16[128,2048]{1,0:T(8,128)(2,1)S(1)} %pad_maximum_fusion.1.refs_0_), channel_id=1, source_target_pairs={{0,4},{4,0},{8,12},{12,8},{16,20},{20,16},{24,28},{28,24},{1,5},{5... | collective-permute-start | bytes 1572872 | tf_op jit(solution)/shard_map/ppermute | solution.py:197
  24.7 12.0 %collective-permute-start.11 = (bf16[128,1024]{1,0:T(8,128)(2,1)S(1)}, bf16[128,1024]{1,0:T(8,128)(2,1)S(1)}, u32[]{:S(2)}, u32[]{:S(2)}) collective-permute-start(bf16[128,1024]{1,0:T(8,128)(2,1)S(1)} %collective-permute-done.2.refs_1_), channel_id=1, source_target_pairs={{0,24},{4,28},{8,0},{12,4},{16,8},{20,12},{24,16},{28,20},{1,25},{... | collective-permute-start | bytes 786440 | tf_op jit(solution)/shard_map/ppermute | solution.py:199
  25.9 11.8 %collective-permute-start.14 = (bf16[128,1024]{1,0:T(8,128)(2,1)S(1)}, bf16[128,1024]{1,0:T(8,128)(2,1)S(1)}, u32[]{:S(2)}, u32[]{:S(2)}) collective-permute-start(bf16[128,1024]{1,0:T(8,128)(2,1)S(1)} %collective-permute-done.2.refs_1_), channel_id=1, source_target_pairs={{0,8},{4,12},{8,16},{12,20},{16,24},{20,28},{24,0},{28,4},{1,9},{5... | collective-permute-start | bytes 786440 | tf_op jit(solution)/shard_map/ppermute | solution.py:198
  41.0 211.1 %reduce-scatter.2.cloned.1.call-start = ((), (), s32[]{:S(2)}) async-start(), calls=%async_computation.3 | async-start | bytes 2621440 | tf_op jit(solution)/shard_map/reduce_scatter | solution.py:278
  41.1 12.8 %collective-permute-start.6 = (bf16[128,2048]{1,0:T(8,128)(2,1)S(1)}, bf16[128,2048]{1,0:T(8,128)(2,1)S(1)}, u32[]{:S(2)}, u32[]{:S(2)}) collective-permute-start(bf16[128,2048]{1,0:T(8,128)(2,1)S(1)} %pad_maximum_fusion.2.refs_0_), channel_id=1, source_target_pairs={{0,4},{4,0},{8,12},{12,8},{16,20},{20,16},{24,28},{28,24},{1,5},{5... | collective-permute-start | bytes 1572872 | tf_op jit(solution)/shard_map/ppermute | solution.py:197
  42.6 22.6 %collective-permute-start.4 = (bf16[128,2048]{1,0:T(8,128)(2,1)S(1)}, bf16[128,2048]{1,0:T(8,128)(2,1)S(1)}, u32[]{:S(2)}, u32[]{:S(2)}) collective-permute-start(bf16[128,2048]{1,0:T(8,128)(2,1)S(1)} %pad_maximum_fusion.refs_0_), channel_id=1, source_target_pairs={{0,4},{4,0},{8,12},{12,8},{16,20},{20,16},{24,28},{28,24},{1,5},{5... | collective-permute-start | bytes 1572872 | tf_op jit(solution)/shard_map/ppermute | solution.py:197
  44.3 6.7 %collective-permute-start.12 = (bf16[128,1024]{1,0:T(8,128)(2,1)S(1)}, bf16[128,1024]{1,0:T(8,128)(2,1)S(1)}, u32[]{:S(2)}, u32[]{:S(2)}) collective-permute-start(bf16[128,1024]{1,0:T(8,128)(2,1)S(1)} %collective-permute-done.refs_6_), channel_id=1, source_target_pairs={{0,8},{4,12},{8,16},{12,20},{16,24},{20,28},{24,0},{28,4},{1,9},{5... | collective-permute-start | bytes 786440 | tf_op jit(solution)/shard_map/ppermute | solution.py:198
  45.0 6.7 %collective-permute-start.15 = (bf16[128,1024]{1,0:T(8,128)(2,1)S(1)}, bf16[128,1024]{1,0:T(8,128)(2,1)S(1)}, u32[]{:S(2)}, u32[]{:S(2)}) collective-permute-start(bf16[128,1024]{1,0:T(8,128)(2,1)S(1)} %collective-permute-done.11.refs_3_), channel_id=1, source_target_pairs={{0,24},{4,28},{8,0},{12,4},{16,8},{20,12},{24,16},{28,20},{1,25},{... | collective-permute-start | bytes 786440 | tf_op jit(solution)/shard_map/ppermute | solution.py:199
  72.5 5.6 %collective-permute-start.16 = (bf16[256,1024]{1,0:T(8,128)(2,1)S(1)}, bf16[256,1024]{1,0:T(8,128)(2,1)S(1)}, u32[]{:S(2)}, u32[]{:S(2)}) collective-permute-start(bf16[256,1024]{1,0:T(8,128)(2,1)S(1)} %get-tuple-element.101), channel_id=1, source_target_pairs={{0,32},{32,0},{64,96},{96,64},{1,33},{33,1},{65,97},{97,65},{2,34}... | collective-permute-start | bytes 1572872 | tf_op jit(solution)/shard_map/ppermute | solution.py:260
  75.7 25.2 %collective-permute-start.8 = (bf16[128,2048]{1,0:T(8,128)(2,1)S(1)}, bf16[128,2048]{1,0:T(8,128)(2,1)S(1)}, u32[]{:S(2)}, u32[]{:S(2)}) collective-permute-start(bf16[128,2048]{1,0:T(8,128)(2,1)S(1)} %copy-done.16), channel_id=1, source_target_pairs={{0,24},{4,28},{8,0},{12,4},{16,8},{20,12},{24,16},{28,20},{1,25},{... | collective-permute-start | bytes 1572872 | tf_op jit(solution)/shard_map/ppermute | solution.py:199
  78.1 26.2 %collective-permute-start.7 = (bf16[128,2048]{1,0:T(8,128)(2,1)S(1)}, bf16[128,2048]{1,0:T(8,128)(2,1)S(1)}, u32[]{:S(2)}, u32[]{:S(2)}) collective-permute-start(bf16[128,2048]{1,0:T(8,128)(2,1)S(1)} %copy-done.16), channel_id=1, source_target_pairs={{0,8},{4,12},{8,16},{12,20},{16,24},{20,28},{24,0},{28,4},{1,9},{5... | collective-permute-start | bytes 1572872 | tf_op jit(solution)/shard_map/ppermute | solution.py:198
  78.3 26.8 %collective-permute-start.23 = (bf16[256,1024]{1,0:T(8,128)(2,1)S(1)}, bf16[256,1024]{1,0:T(8,128)(2,1)}, u32[]{:S(2)}, u32[]{:S(2)}) collective-permute-start(bf16[256,1024]{1,0:T(8,128)(2,1)S(1)} %add_convert_fusion.3), channel_id=1, source_target_pairs={{0,64},{32,96},{64,0},{96,32},{1,65},{33,97},{65,1},{97,33},{2,66}... | collective-permute-start | bytes 1572872 | tf_op jit(solution)/shard_map/ppermute | solution.py:263
  107.7 24.6 %copy-start.2 = (bf16[1024,2048]{1,0:T(8,128)(2,1)S(1)}, bf16[1024,2048]{1,0:T(8,128)(2,1)}, u32[]{:S(2)}) copy-start(bf16[1024,2048]{1,0:T(8,128)(2,1)} %all-gather.5.cloned.1.call-done.refs_0_) | copy-start | bytes 12582916
  107.7 24.6 %copy-start.4 = (f32[1024,1024]{1,0:T(8,128)S(1)}, f32[1024,1024]{1,0:T(8,128)}, u32[]{:S(2)}) copy-start(f32[1024,1024]{1,0:T(8,128)} %copy-done.3) | copy-start | bytes 12582916
  114.3 3.4 %collective-permute-start.24 = (bf16[256,2048]{1,0:T(8,128)(2,1)S(1)}, bf16[256,2048]{1,0:T(8,128)(2,1)S(1)}, u32[]{:S(2)}, u32[]{:S(2)}) collective-permute-start(bf16[256,2048]{1,0:T(8,128)(2,1)S(1)} %get-tuple-element.115), channel_id=1, source_target_pairs={{0,32},{32,0},{64,96},{96,64},{1,33},{33,1},{65,97},{97,65},{2,34}... | collective-permute-start | bytes 3145736 | tf_op jit(solution)/shard_map/ppermute | solution.py:260
  115.0 14.7 %collective-permute-start.10 = (bf16[128,2048]{1,0:T(8,128)(2,1)S(1)}, bf16[128,2048]{1,0:T(8,128)(2,1)S(1)}, u32[]{:S(2)}, u32[]{:S(2)}) collective-permute-start(bf16[128,2048]{1,0:T(8,128)(2,1)S(1)} %pad_maximum_fusion.refs_0_), channel_id=1, source_target_pairs={{0,8},{4,12},{8,16},{12,20},{16,24},{20,28},{24,0},{28,4},{1,9},{5... | collective-permute-start | bytes 1572872 | tf_op jit(solution)/shard_map/ppermute | solution.py:198
  115.6 14.1 %collective-permute-start.17 = (bf16[128,2048]{1,0:T(8,128)(2,1)}, bf16[128,2048]{1,0:T(8,128)(2,1)S(1)}, u32[]{:S(2)}, u32[]{:S(2)}) collective-permute-start(bf16[128,2048]{1,0:T(8,128)(2,1)} %copy-done.22), channel_id=1, source_target_pairs={{0,24},{4,28},{8,0},{12,4},{16,8},{20,12},{24,16},{28,20},{1,25},{... | collective-permute-start | bytes 1572872 | tf_op jit(solution)/shard_map/ppermute | solution.py:199
  118.1 34.1 %copy-start.11 = (bf16[128,2048]{1,0:T(8,128)(2,1)S(1)}, bf16[128,2048]{1,0:T(8,128)(2,1)}, u32[]{:S(2)}) copy-start(bf16[128,2048]{1,0:T(8,128)(2,1)} %copy-done.10) | copy-start | bytes 1572868
  118.1 34.1 %copy-start.17 = (bf16[128,2048]{1,0:T(8,128)(2,1)S(1)}, bf16[128,2048]{1,0:T(8,128)(2,1)}, u32[]{:S(2)}) copy-start(bf16[128,2048]{1,0:T(8,128)(2,1)} %copy-done.15) | copy-start | bytes 1572868
  118.2 34.1 %copy-start.23 = (bf16[128,2048]{1,0:T(8,128)(2,1)S(1)}, bf16[128,2048]{1,0:T(8,128)(2,1)}, u32[]{:S(2)}) copy-start(bf16[128,2048]{1,0:T(8,128)(2,1)} %copy-done.22) | copy-start | bytes 1572868
  118.2 34.1 %copy-start.25 = (bf16[128,2048]{1,0:T(8,128)(2,1)S(1)}, bf16[128,2048]{1,0:T(8,128)(2,1)}, u32[]{:S(2)}) copy-start(bf16[128,2048]{1,0:T(8,128)(2,1)} %copy-done.24) | copy-start | bytes 1572868
  118.2 34.1 %collective-permute-start.25 = (bf16[256,2048]{1,0:T(8,128)(2,1)S(1)}, bf16[256,2048]{1,0:T(8,128)(2,1)S(1)}, u32[]{:S(2)}, u32[]{:S(2)}) collective-permute-start(bf16[256,2048]{1,0:T(8,128)(2,1)S(1)} %add_convert_fusion.2), channel_id=1, source_target_pairs={{0,64},{32,96},{64,0},{96,32},{1,65},{33,97},{65,1},{97,33},{2,66}... | collective-permute-start | bytes 3145736 | tf_op jit(solution)/shard_map/ppermute | solution.py:263
  119.5 22.0 %collective-permute-start.22 = (bf16[128,2048]{1,0:T(8,128)(2,1)S(1)}, bf16[128,2048]{1,0:T(8,128)(2,1)S(1)}, u32[]{:S(2)}, u32[]{:S(2)}) collective-permute-start(bf16[128,2048]{1,0:T(8,128)(2,1)S(1)} %copy-done.9), channel_id=1, source_target_pairs={{0,8},{4,12},{8,16},{12,20},{16,24},{20,28},{24,0},{28,4},{1,9},{5... | collective-permute-start | bytes 1572872 | tf_op jit(solution)/shard_map/ppermute | solution.py:198
  119.7 21.8 %collective-permute-start.9 = (bf16[128,2048]{1,0:T(8,128)(2,1)S(1)}, bf16[128,2048]{1,0:T(8,128)(2,1)S(1)}, u32[]{:S(2)}, u32[]{:S(2)}) collective-permute-start(bf16[128,2048]{1,0:T(8,128)(2,1)S(1)} %pad_maximum_fusion.refs_0_), channel_id=1, source_target_pairs={{0,24},{4,28},{8,0},{12,4},{16,8},{20,12},{24,16},{28,20},{1,25},{... | collective-permute-start | bytes 1572872 | tf_op jit(solution)/shard_map/ppermute | solution.py:199
  129.7 45.5 %copy-start.18 = (bf16[128,2048]{1,0:T(8,128)(2,1)}, bf16[128,2048]{1,0:T(8,128)(2,1)S(1)}, u32[]{:S(2)}) copy-start(bf16[128,2048]{1,0:T(8,128)(2,1)S(1)} %collective-permute-done.10.refs_6_) | copy-start | bytes 1572868
  129.8 21.7 %collective-permute-start.18 = (bf16[128,2048]{1,0:T(8,128)(2,1)S(1)}, bf16[128,2048]{1,0:T(8,128)(2,1)S(1)}, u32[]{:S(2)}, u32[]{:S(2)}) collective-permute-start(bf16[128,2048]{1,0:T(8,128)(2,1)S(1)} %copy-done.13), channel_id=1, source_target_pairs={{0,24},{4,28},{8,0},{12,4},{16,8},{20,12},{24,16},{28,20},{1,25},{... | collective-permute-start | bytes 1572872 | tf_op jit(solution)/shard_map/ppermute | solution.py:199
  132.3 19.9 %collective-permute-start.21 = (bf16[128,2048]{1,0:T(8,128)(2,1)S(1)}, bf16[128,2048]{1,0:T(8,128)(2,1)S(1)}, u32[]{:S(2)}, u32[]{:S(2)}) collective-permute-start(bf16[128,2048]{1,0:T(8,128)(2,1)S(1)} %copy-done.13), channel_id=1, source_target_pairs={{0,8},{4,12},{8,16},{12,20},{16,24},{20,28},{24,0},{28,4},{1,9},{5... | collective-permute-start | bytes 1572872 | tf_op jit(solution)/shard_map/ppermute | solution.py:198
  141.5 33.7 %copy-start.20 = (bf16[128,2048]{1,0:T(8,128)(2,1)}, bf16[128,2048]{1,0:T(8,128)(2,1)S(1)}, u32[]{:S(2)}) copy-start(bf16[128,2048]{1,0:T(8,128)(2,1)S(1)} %collective-permute-done.9.refs_2_) | copy-start | bytes 1572868
  151.5 23.8 %copy-start.26 = (bf16[128,2048]{1,0:T(8,128)(2,1)}, bf16[128,2048]{1,0:T(8,128)(2,1)S(1)}, u32[]{:S(2)}) copy-start(bf16[128,2048]{1,0:T(8,128)(2,1)S(1)} %collective-permute-done.18.refs_3_) | copy-start | bytes 1572868
  159.3 4.2 %collective-permute-start.26 = (bf16[256,2048]{1,0:T(8,128)(2,1)S(1)}, bf16[256,2048]{1,0:T(8,128)(2,1)S(1)}, u32[]{:S(2)}, u32[]{:S(2)}) collective-permute-start(bf16[256,2048]{1,0:T(8,128)(2,1)S(1)} %get-tuple-element.126), channel_id=1, source_target_pairs={{0,32},{32,0},{64,96},{96,64},{1,33},{33,1},{65,97},{97,65},{2,34}... | collective-permute-start | bytes 3145736 | tf_op jit(solution)/shard_map/ppermute | solution.py:260
  160.1 15.1 %collective-permute-start.19 = (bf16[128,2048]{1,0:T(8,128)(2,1)S(1)}, bf16[128,2048]{1,0:T(8,128)(2,1)S(1)}, u32[]{:S(2)}, u32[]{:S(2)}) collective-permute-start(bf16[128,2048]{1,0:T(8,128)(2,1)S(1)} %collective-permute-done.10.refs_6_), channel_id=1, source_target_pairs={{0,8},{4,12},{8,16},{12,20},{16,24},{20,28},{24,0},{28,4},{1,9},{5... | collective-permute-start | bytes 1572872 | tf_op jit(solution)/shard_map/ppermute | solution.py:198
  160.6 14.6 %collective-permute-start.20 = (bf16[128,2048]{1,0:T(8,128)(2,1)S(1)}, bf16[128,2048]{1,0:T(8,128)(2,1)S(1)}, u32[]{:S(2)}, u32[]{:S(2)}) collective-permute-start(bf16[128,2048]{1,0:T(8,128)(2,1)S(1)} %collective-permute-done.18.refs_3_), channel_id=1, source_target_pairs={{0,24},{4,28},{8,0},{12,4},{16,8},{20,12},{24,16},{28,20},{1,25},{... | collective-permute-start | bytes 1572872 | tf_op jit(solution)/shard_map/ppermute | solution.py:199
  163.0 27.4 %collective-permute-start.28 = (bf16[256,2048]{1,0:T(8,128)(2,1)}, bf16[256,2048]{1,0:T(8,128)(2,1)}, u32[]{:S(2)}, u32[]{:S(2)}) collective-permute-start(bf16[256,2048]{1,0:T(8,128)(2,1)} %get-tuple-element.144), channel_id=1, source_target_pairs={{0,32},{32,0},{64,96},{96,64},{1,33},{33,1},{65,97},{97,65},{2,34}... | collective-permute-start | bytes 3145736 | tf_op jit(solution)/shard_map/ppermute | solution.py:261
  186.5 2.2 collective-permute-start.27
  187.2 25.1 %collective-permute-start.30 = (bf16[256,2048]{1,0:T(8,128)(2,1)}, bf16[256,2048]{1,0:T(8,128)(2,1)S(1)}, u32[]{:S(2)}, u32[]{:S(2)}) collective-permute-start(bf16[256,2048]{1,0:T(8,128)(2,1)} %add_convert_fusion.1), channel_id=1, source_target_pairs={{0,64},{32,96},{64,0},{96,32},{1,65},{33,97},{65,1},{97,33},{2,66}... | collective-permute-start | bytes 3145736 | tf_op jit(solution)/shard_map/ppermute | solution.py:263
  194.0 25.3 %copy-start.58 = (bf16[256,3584]{1,0:T(8,128)(2,1)}, bf16[256,3584]{1,0:T(8,128)(2,1)S(1)}, u32[]{:S(2)}) copy-start(bf16[256,3584]{1,0:T(8,128)(2,1)S(1)} %get-tuple-element.145) | copy-start | bytes 5505028
  194.0 25.2 %copy-start.59 = (bf16[256,3584]{1,0:T(8,128)(2,1)}, bf16[256,3584]{1,0:T(8,128)(2,1)S(1)}, u32[]{:S(2)}) copy-start(bf16[256,3584]{1,0:T(8,128)(2,1)S(1)} %get-tuple-element.147) | copy-start | bytes 5505028
  219.2 3.6 %collective-permute-start.32 = (bf16[256,2048]{1,0:T(8,128)(2,1)S(1)}, bf16[256,2048]{1,0:T(8,128)(2,1)S(1)}, u32[]{:S(2)}, u32[]{:S(2)}) collective-permute-start(bf16[256,2048]{1,0:T(8,128)(2,1)S(1)} %get-tuple-element.158), channel_id=1, source_target_pairs={{0,32},{32,0},{64,96},{96,64},{1,33},{33,1},{65,97},{97,65},{2,34}... | collective-permute-start | bytes 3145736 | tf_op jit(solution)/shard_map/ppermute | solution.py:260
  220.0 5.5 %collective-permute-start.29 = (bf16[256,2048]{1,0:T(8,128)(2,1)}, bf16[256,2048]{1,0:T(8,128)(2,1)}, u32[]{:S(2)}, u32[]{:S(2)}) collective-permute-start(bf16[256,2048]{1,0:T(8,128)(2,1)} %get-tuple-element.146), channel_id=1, source_target_pairs={{0,32},{32,0},{64,96},{96,64},{1,33},{33,1},{65,97},{97,65},{2,34}... | collective-permute-start | bytes 3145736 | tf_op jit(solution)/shard_map/ppermute | solution.py:261
  220.1 8.7 %collective-permute-start.31 = (bf16[256,2048]{1,0:T(8,128)(2,1)}, bf16[256,2048]{1,0:T(8,128)(2,1)}, u32[]{:S(2)}, u32[]{:S(2)}) collective-permute-start(bf16[256,2048]{1,0:T(8,128)(2,1)} %get-tuple-element.157), channel_id=1, source_target_pairs={{0,32},{32,0},{64,96},{96,64},{1,33},{33,1},{65,97},{97,65},{2,34}... | collective-permute-start | bytes 3145736 | tf_op jit(solution)/shard_map/ppermute | solution.py:261
  224.2 24.7 %collective-permute-start.33 = (bf16[256,2048]{1,0:T(8,128)(2,1)}, bf16[256,2048]{1,0:T(8,128)(2,1)}, u32[]{:S(2)}, u32[]{:S(2)}) collective-permute-start(bf16[256,2048]{1,0:T(8,128)(2,1)} %add_convert_fusion), channel_id=1, source_target_pairs={{0,64},{32,96},{64,0},{96,32},{1,65},{33,97},{65,1},{97,33},{2,66}... | collective-permute-start | bytes 3145736 | tf_op jit(solution)/shard_map/ppermute | solution.py:263
  (54 other events, 353.5 us)
Sparse Core Ops, SparseCore 0:
  9.7 34.0 all-gather.2
  46.0 59.5 all-gather.4
  185.6 30.8 reduce-scatter.1
